TPU v7x, 32 devices: a whole 2x2x4 slice. The times are simulated.
32 devices in a mesh: grp: 2 (over y), pair: 4 (over z), dir: 2 (over x), pol: 2 (over core).
Axes of the slice: x: 2, y: 2, z: 4, core: 2. Of those that a mesh axis runs over, the one named last changes fastest.
Arguments:
- blocks: int32 [40, 2], P(('grp', 'pair')), parts along dimension 0, may hold values from 0 to 3, as said below
- counts: int32 [8], P(('grp', 'pair')), parts along dimension 0, may hold values from 1 to 5, as said below
- gains: float32 [16, 2, 8, 512], P(('grp', 'dir'), None, None, 'pair'), parts along dimension 0, may hold values from -1.5 to 1.5
- coherency: bfloat16 [40, 2, 8, 2, 8, 16384], P(('grp', 'pair'), 'pol', 'dir'), parts along dimension 0, may hold values from -6 to 6
- observed: bfloat16 [40, 2, 2, 8, 16384], P(('grp', 'pair'), 'pol'), parts along dimension 0, may hold values from -6 to 6
Outputs:
- residual: bfloat16 [40, 2, 2, 8, 16384], P(('grp', 'pair'), 'pol'), parts along dimension 0
- gradient: float32 [16, 2, 8, 512], P(('grp', 'dir'), None, None, ('pair', 'pol')), parts along dimension 0
There are 2 independent parts, one for each index of `grp`. A program takes and returns all parts, laid end to end along the dimension named above; each array names one. Nothing has to cross between parts.
Inputs may be any that keep to these rules, and one draw needn't show every extreme that they name: `blocks`: over the used slots every block pair (a, b) with a <= b appears exactly once, a <= b; an unused slot repeats the last used pair of its pair index. `counts`: they sum to 10; some pair index uses all 5 slots.
All inputs are finite; a program needn't handle non-finite values.
Results may differ from a plain program's by a relative error of at most 0.007.
Values may be sent and summed in bfloat16 or wider, within the bound.
A program may use at most 384 MiB of HBM per device.

v0:
```python
import jax
import jax.numpy as jnp
from jax import lax
from jax.sharding import PartitionSpec as P


def split_parts(matrix, axis):
    return [lax.index_in_dim(matrix, c, axis, keepdims=False) for c in range(8)]


def product(left, right):
    result = [None] * 8
    for row_index in range(2):
        for col_index in range(2):
            real_sum = 0.0
            imag_sum = 0.0
            for mid_index in range(2):
                left_re = left[2 * row_index + mid_index]
                left_im = left[4 + 2 * row_index + mid_index]
                right_re = right[2 * mid_index + col_index]
                right_im = right[4 + 2 * mid_index + col_index]
                real_sum = real_sum + left_re * right_re - left_im * right_im
                imag_sum = imag_sum + left_re * right_im + left_im * right_re
            result[2 * row_index + col_index] = real_sum
            result[4 + 2 * row_index + col_index] = imag_sum
    return result


def adjoint(matrix):
    return [
        matrix[0],
        matrix[2],
        matrix[1],
        matrix[3],
        -matrix[4],
        -matrix[6],
        -matrix[5],
        -matrix[7],
    ]


def direction_gains(one_dir, first, second, nblocks, blk):
    table = one_dir.reshape(one_dir.shape[0], 8, nblocks, blk)
    gain_a = jnp.moveaxis(jnp.take(table, first, axis=2), 2, 0)
    gain_b = jnp.moveaxis(jnp.take(table, second, axis=2), 2, 0)
    left_g = jnp.repeat(gain_a, blk, axis=3)[:, None]
    right_g = jnp.tile(gain_b, (1, 1, 1, blk))[:, None]
    return (split_parts(left_g, 3), split_parts(right_g, 3))


def baseline_mask(first, second, used, blk):
    pair_index = jnp.arange(blk * blk)
    upper = pair_index // blk < pair_index % blk
    keep = used[:, None] & ((first < second)[:, None] | upper[None, :])
    return keep.astype(jnp.float32)[:, None, None, None, :]


def body(blocks, counts, gains, coherency, observed):
    nblocks = lax.axis_size("pair")
    dir_local = gains.shape[0]
    chans = gains.shape[1]
    blk = gains.shape[3]
    maxb = blocks.shape[0]
    whole = lax.all_gather(gains, "pair", axis=3, tiled=True)
    first = blocks[:, 0]
    second = blocks[:, 1]
    used = jnp.arange(maxb) < counts[0]
    mask = baseline_mask(first, second, used, blk)
    partial_sum = jnp.zeros(observed.shape, jnp.float32)
    for local in range(dir_local):
        left_g, right_g = direction_gains(whole[local], first, second, nblocks, blk)
        model_c = split_parts(coherency[:, :, local].astype(jnp.float32), 3)
        partial_sum = partial_sum + jnp.stack(
            product(product(left_g, model_c), adjoint(right_g)), axis=3
        )
    predicted = lax.psum(partial_sum.astype(jnp.bfloat16), "dir").astype(jnp.float32)
    residual = (mask * (observed.astype(jnp.float32) - predicted)).astype(jnp.bfloat16)
    resid_parts = split_parts(residual.astype(jnp.float32), 3)
    onehot_first = (first[:, None] == jnp.arange(nblocks)[None, :]).astype(jnp.float32)
    onehot_second = (second[:, None] == jnp.arange(nblocks)[None, :]).astype(jnp.float32)
    grads = []
    for local in range(dir_local):
        left_g, right_g = direction_gains(whole[local], first, second, nblocks, blk)
        model_c = split_parts(coherency[:, :, local].astype(jnp.float32), 3)
        toward_first = jnp.stack(product(resid_parts, product(right_g, adjoint(model_c))), axis=3)
        toward_second = jnp.stack(product(adjoint(resid_parts), product(left_g, model_c)), axis=3)
        toward_first = jnp.sum(toward_first, axis=1).reshape(maxb, chans, 8, blk, blk).sum(axis=4)
        toward_second = jnp.sum(toward_second, axis=1).reshape(maxb, chans, 8, blk, blk).sum(axis=3)
        grad_dir = jnp.einsum(
            "scxb,sn->cxnb", toward_first, onehot_first, precision=lax.Precision.HIGHEST
        )
        grad_dir = grad_dir + jnp.einsum(
            "scxb,sn->cxnb", toward_second, onehot_second, precision=lax.Precision.HIGHEST
        )
        grads.append(grad_dir.reshape(chans, 8, nblocks * blk))
    gradient = jnp.stack(grads, axis=0)
    owned = lax.psum_scatter(gradient, ("pair", "pol"), scatter_dimension=3, tiled=True)
    return (residual, owned)


def solution(mesh):
    in_specs = (
        P(("grp", "pair"), None),
        P(("grp", "pair")),
        P(("grp", "dir"), None, None, "pair"),
        P(("grp", "pair"), "pol", "dir", None, None, None),
        P(("grp", "pair"), "pol", None, None, None),
    )
    out_specs = (
        P(("grp", "pair"), "pol", None, None, None),
        P(("grp", "dir"), None, None, ("pair", "pol")),
    )
    return jax.shard_map(body, mesh=mesh, in_specs=in_specs, out_specs=out_specs, check_vma=False)
```

profile of v0, /device:TPU:0, one launch (start us, length us, event | category | flops | bytes accessed | tf_op | source)
XLA Modules:
  0.0 969.8 jit_solution(4644786704517554444)
XLA Ops:
  8.0 15.3 %all_gather.3 = f32[4,2,8,512]{3,2,1,0:T(8,128)S(1)} all-gather(f32[4,2,8,128]{3,2,1,0:T(8,128)} %param.9), channel_id=1, replica_groups=mesh['grp'=2,'pair'=4,'dir'=2,'pol'=2] {'pair'}, dimensions={3}, use_global_device_ids=true | all-gather | bytes 163840 | tf_op jit(solution)/shard_map/all_gather | solution.py:64
  31.2 6.8 tile.19
  38.0 18.1 %fusion.489 = (f32[5,1,2,1,16384]{4,3,2,0,1:T(1,128)S(1)}, f32[5,1,2,1,16384]{4,3,2,0,1:T(1,128)}, f32[5,1,2,1,16384]{4,3,2,0,1:T(1,128)}, f32[5,1,2,1,16384]{4,...) fusion(f32[5,1,2,8,16384]{4,3,2,0,1:T(8,128)} %tile.19), kind=kLoop, calls=%fused_computation.929 | loop fusion | bytes 10485760 | tf_op jit(solution)/shard_map/slice | solution.py:8
  56.1 3.3 broadcast_in_dim.18
  59.4 6.9 broadcast_in_dim_reshape.17
  66.3 17.8 %fusion.488 = (f32[5,1,2,1,16384]{4,3,2,0,1:T(1,128)}, f32[5,1,2,1,16384]{4,3,2,0,1:T(1,128)}, f32[5,1,2,1,16384]{4,3,2,0,1:T(1,128)}, f32[5,1,2,1,16384]{4,3,2,...) fusion(f32[5,1,2,8,16384]{4,3,2,0,1:T(8,128)} %broadcast_in_dim, ...), kind=kLoop, calls=%fused_computation.928 | loop fusion | bytes 10485760 | tf_op jit(solution)/shard_map/slice | solution.py:8
  84.1 7.7 fusion.487
  91.8 9.2 fusion.2
  101.0 9.2 fusion.153
  113.4 6.2 fusion.155
  134.3 6.8 tile.17
  141.1 18.3 %fusion.491 = (f32[5,1,2,1,16384]{4,3,2,0,1:T(1,128)S(1)}, f32[5,1,2,1,16384]{4,3,2,0,1:T(1,128)}, f32[5,1,2,1,16384]{4,3,2,0,1:T(1,128)}, f32[5,1,2,1,16384]{4,...) fusion(f32[5,1,2,8,16384]{4,3,2,0,1:T(8,128)} %tile.17), kind=kLoop, calls=%fused_computation.931 | loop fusion | bytes 10485760 | tf_op jit(solution)/shard_map/slice | solution.py:8
  159.5 3.3 broadcast_in_dim.17
  162.7 6.8 broadcast_in_dim_reshape.16
  169.6 17.7 %fusion.490 = (f32[5,1,2,1,16384]{4,3,2,0,1:T(1,128)S(1)}, f32[5,1,2,1,16384]{4,3,2,0,1:T(1,128)S(1)}, f32[5,1,2,1,16384]{4,3,2,0,1:T(1,128)S(1)}, f32[5,1,2,1,1...) fusion(f32[5,1,2,8,16384]{4,3,2,0,1:T(8,128)} %broadcast_in_dim, ...), kind=kLoop, calls=%fused_computation.930 | loop fusion | bytes 10485760 | tf_op jit(solution)/shard_map/slice | solution.py:8
  187.3 7.8 fusion.185
  196.9 6.6 fusion.187
  212.3 3.2 copy-done.138
  218.2 6.8 tile.21
  225.0 17.9 %fusion.493 = (f32[5,1,2,1,16384]{4,3,2,0,1:T(1,128)}, f32[5,1,2,1,16384]{4,3,2,0,1:T(1,128)}, f32[5,1,2,1,16384]{4,3,2,0,1:T(1,128)}, f32[5,1,2,1,16384]{4,3,2,...) fusion(f32[5,1,2,8,16384]{4,3,2,0,1:T(8,128)} %tile.21), kind=kLoop, calls=%fused_computation.933 | loop fusion | bytes 10485760 | tf_op jit(solution)/shard_map/slice | solution.py:8
  246.1 6.8 broadcast_in_dim_reshape.18
  252.9 17.9 %fusion.492 = (f32[5,1,2,1,16384]{4,3,2,0,1:T(1,128)}, f32[5,1,2,1,16384]{4,3,2,0,1:T(1,128)}, f32[5,1,2,1,16384]{4,3,2,0,1:T(1,128)}, f32[5,1,2,1,16384]{4,3,2,...) fusion(f32[5,1,2,8,16384]{4,3,2,0,1:T(8,128)} %broadcast_in_dim, ...), kind=kLoop, calls=%fused_computation.932 | loop fusion | bytes 10485760 | tf_op jit(solution)/shard_map/slice | solution.py:8
  270.8 8.4 fusion
  279.2 9.4 fusion.121
  291.5 6.5 fusion.123
  306.7 3.3 copy-done.139
  312.6 6.8 tile.23
  319.4 17.7 %fusion.495 = (f32[5,1,2,1,16384]{4,3,2,0,1:T(1,128)}, f32[5,1,2,1,16384]{4,3,2,0,1:T(1,128)}, f32[5,1,2,1,16384]{4,3,2,0,1:T(1,128)}, f32[5,1,2,1,16384]{4,3,2,...) fusion(f32[5,1,2,8,16384]{4,3,2,0,1:T(8,128)} %tile.23), kind=kLoop, calls=%fused_computation.935 | loop fusion | bytes 10485760 | tf_op jit(solution)/shard_map/slice | solution.py:8
  337.1 3.2 broadcast_in_dim.34
  340.3 6.8 broadcast_in_dim_reshape.19
  347.2 17.9 %fusion.494 = (f32[5,1,2,1,16384]{4,3,2,0,1:T(1,128)}, f32[5,1,2,1,16384]{4,3,2,0,1:T(1,128)}, f32[5,1,2,1,16384]{4,3,2,0,1:T(1,128)}, f32[5,1,2,1,16384]{4,3,2,...) fusion(f32[5,1,2,8,16384]{4,3,2,0,1:T(8,128)} %broadcast_in_dim, ...), kind=kLoop, calls=%fused_computation.934 | loop fusion | bytes 10485760 | tf_op jit(solution)/shard_map/slice | solution.py:8
  365.2 8.7 fusion.89
  377.4 7.0 fusion.91
  398.1 11.2 %add_convert_fusion = bf16[5,1,2,8,16384]{4,0,3,2,1:T(8,128)(2,1)} fusion(f32[5,1,2,8,16384]{4,0,3,2,1:T(8,128)} %fusion.81, f32[5,1,2,8,16384]{4,0,3,2,1:T(8,128)} %copy-done.139, f32[5,1,2,8,16384]{4,0,3,2,1:T(8,128)} %copy-done.138, f32[5,1,2,8,16384]{4,0,3,2,1:T(8,128)S(1)} %bitcast.249), kind=kLoop, calls=%fused_computation.9 | loop fusion | flops 5242880 | bytes 23592960 | tf_op jit(solution)/shard_map/convert_element_type | solution.py:76
  411.0 107.7 %all-reduce.2.cloned.1.call-done = bf16[5,1,2,8,16384]{4,0,3,2,1:T(8,128)(2,1)} async-done(((bf16[5,1,2,8,16384]{4,0,3,2,1:T(8,128)(2,1)}), bf16[5,1,2,8,16384]{4,0,3,2,1:T(8,128)(2,1)}) %all-reduce.2.cloned.1.call-update) | async-done | bytes 2621456 | tf_op jit(solution)/shard_map/psum | solution.py:76
  518.7 6.6 fusion.454
  532.9 3.7 multiply_subtract_fusion.26
  536.6 4.3 multiply_subtract_fusion.27
  541.1 9.2 multiply_add_fusion.28
  550.4 8.6 multiply_add_fusion.29
  564.7 3.7 multiply_subtract_fusion.18
  568.4 3.4 multiply_subtract_fusion.19
  571.9 9.5 multiply_add_fusion.20
  581.5 8.6 multiply_add_fusion.21
  590.1 4.0 multiply_add_fusion.8
  597.4 9.2 multiply_add_fusion.12
  606.7 8.8 multiply_add_fusion.13
  623.8 9.2 multiply_add_fusion.4
  633.0 8.5 multiply_add_fusion.5
  658.3 6.9 multiply_add_fusion.30
  667.7 5.9 multiply_add_fusion.31
  708.2 4.0 reduce_sum.70
  739.6 7.0 multiply_add_fusion.22
  749.0 5.9 multiply_add_fusion.23
  778.9 4.0 reduce_sum.72
  810.5 7.1 multiply_add_fusion.14
  820.0 5.9 multiply_add_fusion.15
  849.9 4.0 reduce_sum.77
  878.6 3.3 reduce_sum.83
  882.0 7.0 multiply_add_fusion.6
  891.3 5.9 multiply_add_fusion.7
  921.3 3.9 reduce_sum.79
  930.3 5.4 copy.258
  935.7 25.2 %reduce-scatter.4.cloned.1.call-done = f32[64,64]{1,0:T(8,128)} async-done(((f32[512,64]{1,0:T(8,128)}), f32[64,64]{1,0:T(8,128)}) %reduce-scatter.4.cloned.1.call-update) | async-done | bytes 16400
  (719 shorter events, 318.7 us)
Async XLA Ops:
  7.2 511.5 %all-reduce.2.cloned.1.call-start = ((), (), s32[]{:S(2)}) async-start(), calls=%async_computation.1 | async-start | bytes 8388608 | tf_op jit(solution)/shard_map/psum | solution.py:76
  38.0 18.1 %copy-start.237 = (f32[5,2,8,128]{3,2,1,0:T(8,128)S(1)}, f32[5,2,8,128]{3,2,1,0:T(8,128)}, u32[]{:S(2)}) copy-start(f32[5,2,8,128]{3,2,1,0:T(8,128)} %get-tuple-element.236) | copy-start | bytes 122884
  56.1 68.8 %copy-start.63 = (f32[5,1,2,1,16384]{4,3,2,0,1:T(1,128)}, f32[5,1,2,1,16384]{4,3,2,0,1:T(1,128)S(1)}, u32[]{:S(2)}) copy-start(f32[5,1,2,1,16384]{4,3,2,0,1:T(1,128)S(1)} %get-tuple-element.164) | copy-start | bytes 1966084
  56.1 68.8 %copy-start.65 = (f32[5,1,2,1,16384]{4,3,2,0,1:T(1,128)}, f32[5,1,2,1,16384]{4,3,2,0,1:T(1,128)S(1)}, u32[]{:S(2)}) copy-start(f32[5,1,2,1,16384]{4,3,2,0,1:T(1,128)S(1)} %get-tuple-element.165) | copy-start | bytes 1966084
  56.1 68.8 %copy-start.67 = (f32[5,1,2,1,16384]{4,3,2,0,1:T(1,128)}, f32[5,1,2,1,16384]{4,3,2,0,1:T(1,128)S(1)}, u32[]{:S(2)}) copy-start(f32[5,1,2,1,16384]{4,3,2,0,1:T(1,128)S(1)} %get-tuple-element.166) | copy-start | bytes 1966084
  56.1 68.8 %copy-start.69 = (f32[5,1,2,1,16384]{4,3,2,0,1:T(1,128)}, f32[5,1,2,1,16384]{4,3,2,0,1:T(1,128)S(1)}, u32[]{:S(2)}) copy-start(f32[5,1,2,1,16384]{4,3,2,0,1:T(1,128)S(1)} %get-tuple-element.167) | copy-start | bytes 1966084
  56.1 70.5 %copy-start.103 = (f32[5,1,2,1,16384]{4,3,2,0,1:T(1,128)}, f32[5,1,2,1,16384]{4,3,2,0,1:T(1,128)S(1)}, u32[]{:S(2)}) copy-start(f32[5,1,2,1,16384]{4,3,2,0,1:T(1,128)S(1)} %get-tuple-element.161) | copy-start | bytes 1966084
  101.0 11.0 %copy-start.1 = (f32[5,1,2,8,16384]{4,0,3,2,1:T(8,128)}, f32[5,1,2,8,16384]{4,0,3,2,1:T(8,128)S(1)}, u32[]{:S(2)}) copy-start(f32[5,1,2,8,16384]{4,0,3,2,1:T(8,128)S(1)} %get-tuple-element.239) | copy-start | bytes 15728644
  110.2 12.9 %copy-start.3 = (f32[5,1,2,1,16384]{4,0,3,2,1:T(8,128)}, f32[5,1,2,1,16384]{4,0,3,2,1:T(8,128)S(1)}, u32[]{:S(2)}) copy-start(f32[5,1,2,1,16384]{4,0,3,2,1:T(8,128)S(1)} %get-tuple-element.56) | copy-start | bytes 1966084
  110.2 12.9 %copy-start.5 = (f32[5,1,2,1,16384]{4,0,3,2,1:T(8,128)}, f32[5,1,2,1,16384]{4,0,3,2,1:T(8,128)S(1)}, u32[]{:S(2)}) copy-start(f32[5,1,2,1,16384]{4,0,3,2,1:T(8,128)S(1)} %get-tuple-element.57) | copy-start | bytes 1966084
  110.2 12.9 %copy-start.7 = (f32[5,1,2,1,16384]{4,0,3,2,1:T(8,128)}, f32[5,1,2,1,16384]{4,0,3,2,1:T(8,128)S(1)}, u32[]{:S(2)}) copy-start(f32[5,1,2,1,16384]{4,0,3,2,1:T(8,128)S(1)} %get-tuple-element.55) | copy-start | bytes 1966084
  110.2 12.9 %copy-start.9 = (f32[5,1,2,1,16384]{4,0,3,2,1:T(8,128)}, f32[5,1,2,1,16384]{4,0,3,2,1:T(8,128)S(1)}, u32[]{:S(2)}) copy-start(f32[5,1,2,1,16384]{4,0,3,2,1:T(8,128)S(1)} %get-tuple-element.58) | copy-start | bytes 1966084
  159.4 49.4 %copy-start.84 = (f32[5,1,2,1,16384]{4,3,2,0,1:T(1,128)}, f32[5,1,2,1,16384]{4,3,2,0,1:T(1,128)S(1)}, u32[]{:S(2)}) copy-start(f32[5,1,2,1,16384]{4,3,2,0,1:T(1,128)S(1)} %get-tuple-element.180) | copy-start | bytes 1966084
  159.4 49.4 %copy-start.87 = (f32[5,1,2,1,16384]{4,3,2,0,1:T(1,128)}, f32[5,1,2,1,16384]{4,3,2,0,1:T(1,128)S(1)}, u32[]{:S(2)}) copy-start(f32[5,1,2,1,16384]{4,3,2,0,1:T(1,128)S(1)} %get-tuple-element.181) | copy-start | bytes 1966084
  159.4 49.4 %copy-start.90 = (f32[5,1,2,1,16384]{4,3,2,0,1:T(1,128)}, f32[5,1,2,1,16384]{4,3,2,0,1:T(1,128)S(1)}, u32[]{:S(2)}) copy-start(f32[5,1,2,1,16384]{4,3,2,0,1:T(1,128)S(1)} %get-tuple-element.182) | copy-start | bytes 1966084
  159.4 49.4 %copy-start.93 = (f32[5,1,2,1,16384]{4,3,2,0,1:T(1,128)}, f32[5,1,2,1,16384]{4,3,2,0,1:T(1,128)S(1)}, u32[]{:S(2)}) copy-start(f32[5,1,2,1,16384]{4,3,2,0,1:T(1,128)S(1)} %get-tuple-element.183) | copy-start | bytes 1966084
  159.4 51.1 %copy-start.121 = (f32[5,1,2,1,16384]{4,3,2,0,1:T(1,128)}, f32[5,1,2,1,16384]{4,3,2,0,1:T(1,128)S(1)}, u32[]{:S(2)}) copy-start(f32[5,1,2,1,16384]{4,3,2,0,1:T(1,128)S(1)} %get-tuple-element.177) | copy-start | bytes 1966084
  187.2 9.7 slice-start.2
  187.3 9.6 slice-start.3
  195.1 11.9 %copy-start.22 = (f32[5,1,2,1,16384]{4,0,3,2,1:T(8,128)}, f32[5,1,2,1,16384]{4,0,3,2,1:T(8,128)S(1)}, u32[]{:S(2)}) copy-start(f32[5,1,2,1,16384]{4,0,3,2,1:T(8,128)S(1)} %get-tuple-element.66) | copy-start | bytes 1966084
  195.1 11.9 %copy-start.24 = (f32[5,1,2,1,16384]{4,0,3,2,1:T(8,128)}, f32[5,1,2,1,16384]{4,0,3,2,1:T(8,128)S(1)}, u32[]{:S(2)}) copy-start(f32[5,1,2,1,16384]{4,0,3,2,1:T(8,128)S(1)} %get-tuple-element.67) | copy-start | bytes 1966084
  195.1 11.9 %copy-start.30 = (f32[5,1,2,1,16384]{4,0,3,2,1:T(8,128)}, f32[5,1,2,1,16384]{4,0,3,2,1:T(8,128)S(1)}, u32[]{:S(2)}) copy-start(f32[5,1,2,1,16384]{4,0,3,2,1:T(8,128)S(1)} %get-tuple-element.65) | copy-start | bytes 1966084
  195.2 11.9 %copy-start.32 = (f32[5,1,2,1,16384]{4,0,3,2,1:T(8,128)}, f32[5,1,2,1,16384]{4,0,3,2,1:T(8,128)S(1)}, u32[]{:S(2)}) copy-start(f32[5,1,2,1,16384]{4,0,3,2,1:T(8,128)S(1)} %get-tuple-element.68) | copy-start | bytes 1966084
  252.9 17.9 %copy-start.140 = (bf16[5,1,1,2,8,16384]{5,4,3,2,1,0:T(8,128)(2,1)S(1)}, bf16[5,1,1,2,8,16384]{5,4,3,2,1,0:T(8,128)(2,1)}, u32[]{:S(2)}) copy-start(bf16[5,1,1,2,8,16384]{5,4,3,2,1,0:T(8,128)(2,1)} %get-tuple-element.142) | copy-start | bytes 7864324
  279.2 11.3 %copy-start.2 = (f32[5,1,2,8,16384]{4,0,3,2,1:T(8,128)}, f32[5,1,2,8,16384]{4,0,3,2,1:T(8,128)S(1)}, u32[]{:S(2)}) copy-start(f32[5,1,2,8,16384]{4,0,3,2,1:T(8,128)S(1)} %get-tuple-element.238) | copy-start | bytes 15728644
  288.6 12.8 %copy-start.19 = (f32[5,1,2,1,16384]{4,0,3,2,1:T(8,128)}, f32[5,1,2,1,16384]{4,0,3,2,1:T(8,128)S(1)}, u32[]{:S(2)}) copy-start(f32[5,1,2,1,16384]{4,0,3,2,1:T(8,128)S(1)} %get-tuple-element.76) | copy-start | bytes 1966084
  347.1 17.9 %copy-start.95 = (f32[5,1,2,1,16384]{4,3,2,0,1:T(1,128)S(1)}, f32[5,1,2,1,16384]{4,3,2,0,1:T(1,128)}, u32[]{:S(2)}) copy-start(f32[5,1,2,1,16384]{4,3,2,0,1:T(1,128)} %get-tuple-element.212) | copy-start | bytes 1966084
  347.1 17.9 %copy-start.97 = (f32[5,1,2,1,16384]{4,3,2,0,1:T(1,128)S(1)}, f32[5,1,2,1,16384]{4,3,2,0,1:T(1,128)}, u32[]{:S(2)}) copy-start(f32[5,1,2,1,16384]{4,3,2,0,1:T(1,128)} %get-tuple-element.213) | copy-start | bytes 1966084
  347.1 17.9 %copy-start.99 = (f32[5,1,2,1,16384]{4,3,2,0,1:T(1,128)S(1)}, f32[5,1,2,1,16384]{4,3,2,0,1:T(1,128)}, u32[]{:S(2)}) copy-start(f32[5,1,2,1,16384]{4,3,2,0,1:T(1,128)} %get-tuple-element.214) | copy-start | bytes 1966084
  347.1 17.9 %copy-start.101 = (f32[5,1,2,1,16384]{4,3,2,0,1:T(1,128)S(1)}, f32[5,1,2,1,16384]{4,3,2,0,1:T(1,128)}, u32[]{:S(2)}) copy-start(f32[5,1,2,1,16384]{4,3,2,0,1:T(1,128)} %get-tuple-element.215) | copy-start | bytes 1966084
  365.1 11.7 %slice-start.6 = ((s8[8388608]{0:T(1024)(128)(4,1)}), s8[4194304]{0:T(1024)(128)(4,1)S(1)}, s32[]{:S(2)}) async-start(s8[8388608]{0:T(1024)(128)(4,1)} %bitcast.242), calls=%async_computation.9 | async-start | bytes 8388608
  365.1 11.6 %slice-start.7 = ((s8[8388608]{0:T(1024)(128)(4,1)}), s8[4194304]{0:T(1024)(128)(4,1)S(1)}, s32[]{:S(2)}) async-start(s8[8388608]{0:T(1024)(128)(4,1)} %bitcast.242), calls=%async_computation.10 | async-start | bytes 8388608
  373.9 16.1 %copy-start.45 = (f32[5,1,2,1,16384]{4,0,3,2,1:T(8,128)}, f32[5,1,2,1,16384]{4,0,3,2,1:T(8,128)S(1)}, u32[]{:S(2)}) copy-start(f32[5,1,2,1,16384]{4,0,3,2,1:T(8,128)S(1)} %get-tuple-element.86) | copy-start | bytes 1966084
  373.9 16.1 %copy-start.47 = (f32[5,1,2,1,16384]{4,0,3,2,1:T(8,128)}, f32[5,1,2,1,16384]{4,0,3,2,1:T(8,128)S(1)}, u32[]{:S(2)}) copy-start(f32[5,1,2,1,16384]{4,0,3,2,1:T(8,128)S(1)} %get-tuple-element.87) | copy-start | bytes 1966084
  373.9 16.1 %copy-start.49 = (f32[5,1,2,1,16384]{4,0,3,2,1:T(8,128)}, f32[5,1,2,1,16384]{4,0,3,2,1:T(8,128)S(1)}, u32[]{:S(2)}) copy-start(f32[5,1,2,1,16384]{4,0,3,2,1:T(8,128)S(1)} %get-tuple-element.85) | copy-start | bytes 1966084
  373.9 16.1 %copy-start.52 = (f32[5,1,2,1,16384]{4,0,3,2,1:T(8,128)}, f32[5,1,2,1,16384]{4,0,3,2,1:T(8,128)S(1)}, u32[]{:S(2)}) copy-start(f32[5,1,2,1,16384]{4,0,3,2,1:T(8,128)S(1)} %get-tuple-element.88) | copy-start | bytes 1966084
  384.5 10.9 %copy-start.55 = (f32[5,1,2,1,16384]{4,0,3,2,1:T(8,128)}, f32[5,1,2,1,16384]{4,0,3,2,1:T(8,128)S(1)}, u32[]{:S(2)}) copy-start(f32[5,1,2,1,16384]{4,0,3,2,1:T(8,128)S(1)} %get-tuple-element.81) | copy-start | bytes 1966084
  384.5 10.9 %copy-start.57 = (f32[5,1,2,1,16384]{4,0,3,2,1:T(8,128)}, f32[5,1,2,1,16384]{4,0,3,2,1:T(8,128)S(1)}, u32[]{:S(2)}) copy-start(f32[5,1,2,1,16384]{4,0,3,2,1:T(8,128)S(1)} %get-tuple-element.82) | copy-start | bytes 1966084
  384.5 10.9 %copy-start.59 = (f32[5,1,2,1,16384]{4,0,3,2,1:T(8,128)}, f32[5,1,2,1,16384]{4,0,3,2,1:T(8,128)S(1)}, u32[]{:S(2)}) copy-start(f32[5,1,2,1,16384]{4,0,3,2,1:T(8,128)S(1)} %get-tuple-element.80) | copy-start | bytes 1966084
  384.5 10.9 %copy-start.61 = (f32[5,1,2,1,16384]{4,0,3,2,1:T(8,128)}, f32[5,1,2,1,16384]{4,0,3,2,1:T(8,128)S(1)}, u32[]{:S(2)}) copy-start(f32[5,1,2,1,16384]{4,0,3,2,1:T(8,128)S(1)} %get-tuple-element.83) | copy-start | bytes 1966084
  398.1 11.3 %copy-start.239 = (s32[5,2]{0,1:T(2,128)S(1)}, s32[5,2]{0,1:T(2,128)}, u32[]{:S(2)}) copy-start(s32[5,2]{0,1:T(2,128)} %param.7) | copy-start | bytes 124
  409.3 551.6 %reduce-scatter.4.cloned.1.call-start = ((), (), s32[]{:S(2)}) async-start(), calls=%async_computation.2 | async-start | bytes 294912
  525.3 107.7 %copy-start = (f32[5,1,2,8,16384]{4,0,3,2,1:T(8,128)}, f32[5,1,2,8,16384]{4,0,3,2,1:T(8,128)S(1)}, u32[]{:S(2)}) copy-start(f32[5,1,2,8,16384]{4,0,3,2,1:T(8,128)S(1)} %get-tuple-element.47) | copy-start | bytes 15728644
  571.8 9.6 copy-start.64
  571.8 9.6 copy-start.66
  571.8 9.6 copy-start.68
  571.8 9.6 copy-start.70
  581.5 15.0 %slice-start.10 = ((s8[8388608]{0:T(1024)(128)(4,1)}), s8[4194304]{0:T(1024)(128)(4,1)S(1)}, s32[]{:S(2)}) async-start(s8[8388608]{0:T(1024)(128)(4,1)} %bitcast.246), calls=%async_computation.13 | async-start | bytes 8388608
  641.6 13.2 %copy-start.181 = (f32[5,1,2,1,16384]{4,0,3,2,1:T(8,128)S(1)}, f32[5,1,2,1,16384]{4,0,3,2,1:T(8,128)}, u32[]{:S(2)}) copy-start(f32[5,1,2,1,16384]{4,0,3,2,1:T(8,128)} %get-tuple-element.94) | copy-start | bytes 1966084
  646.6 10.6 %copy-start.180 = (f32[5,1,2,1,16384]{4,0,3,2,1:T(8,128)S(1)}, f32[5,1,2,1,16384]{4,0,3,2,1:T(8,128)}, u32[]{:S(2)}) copy-start(f32[5,1,2,1,16384]{4,0,3,2,1:T(8,128)} %get-tuple-element.93) | copy-start | bytes 1966084
  673.6 11.8 %copy-start.184 = (f32[5,1,2,1,16384]{4,0,3,2,1:T(8,128)S(1)}, f32[5,1,2,1,16384]{4,0,3,2,1:T(8,128)}, u32[]{:S(2)}) copy-start(f32[5,1,2,1,16384]{4,0,3,2,1:T(8,128)} %get-tuple-element.99) | copy-start | bytes 1966084
  673.6 13.0 %copy-start.155 = (f32[5,1,2,1,16384]{4,0,3,2,1:T(8,128)S(1)}, f32[5,1,2,1,16384]{4,0,3,2,1:T(8,128)}, u32[]{:S(2)}) copy-start(f32[5,1,2,1,16384]{4,0,3,2,1:T(8,128)} %get-tuple-element.12) | copy-start | bytes 1966084
  676.1 11.7 %copy-start.154 = (f32[5,1,2,1,16384]{4,0,3,2,1:T(8,128)S(1)}, f32[5,1,2,1,16384]{4,0,3,2,1:T(8,128)}, u32[]{:S(2)}) copy-start(f32[5,1,2,1,16384]{4,0,3,2,1:T(8,128)} %get-tuple-element.7) | copy-start | bytes 1966084
  754.8 11.8 %copy-start.185 = (f32[5,1,2,1,16384]{4,0,3,2,1:T(8,128)S(1)}, f32[5,1,2,1,16384]{4,0,3,2,1:T(8,128)}, u32[]{:S(2)}) copy-start(f32[5,1,2,1,16384]{4,0,3,2,1:T(8,128)} %get-tuple-element.111) | copy-start | bytes 1966084
  754.8 13.0 %copy-start.153 = (f32[5,1,2,1,16384]{4,0,3,2,1:T(8,128)S(1)}, f32[5,1,2,1,16384]{4,0,3,2,1:T(8,128)}, u32[]{:S(2)}) copy-start(f32[5,1,2,1,16384]{4,0,3,2,1:T(8,128)} %get-tuple-element.22) | copy-start | bytes 1966084
  757.4 11.7 %copy-start.152 = (f32[5,1,2,1,16384]{4,0,3,2,1:T(8,128)S(1)}, f32[5,1,2,1,16384]{4,0,3,2,1:T(8,128)}, u32[]{:S(2)}) copy-start(f32[5,1,2,1,16384]{4,0,3,2,1:T(8,128)} %get-tuple-element.17) | copy-start | bytes 1966084
  786.9 9.6 copy-start.172
  825.9 11.8 %copy-start.186 = (f32[5,1,2,1,16384]{4,0,3,2,1:T(8,128)S(1)}, f32[5,1,2,1,16384]{4,0,3,2,1:T(8,128)}, u32[]{:S(2)}) copy-start(f32[5,1,2,1,16384]{4,0,3,2,1:T(8,128)} %get-tuple-element.123) | copy-start | bytes 1966084
  825.9 13.0 %copy-start.151 = (f32[5,1,2,1,16384]{4,0,3,2,1:T(8,128)S(1)}, f32[5,1,2,1,16384]{4,0,3,2,1:T(8,128)}, u32[]{:S(2)}) copy-start(f32[5,1,2,1,16384]{4,0,3,2,1:T(8,128)} %get-tuple-element.32) | copy-start | bytes 1966084
  828.5 11.7 %copy-start.150 = (f32[5,1,2,1,16384]{4,0,3,2,1:T(8,128)S(1)}, f32[5,1,2,1,16384]{4,0,3,2,1:T(8,128)}, u32[]{:S(2)}) copy-start(f32[5,1,2,1,16384]{4,0,3,2,1:T(8,128)} %get-tuple-element.27) | copy-start | bytes 1966084
  849.9 9.8 %copy-start.142 = (f32[5,1,2,1,16384]{4,0,3,2,1:T(8,128)S(1)}, f32[5,1,2,1,16384]{4,0,3,2,1:T(8,128)}, u32[]{:S(2)}) copy-start(f32[5,1,2,1,16384]{4,0,3,2,1:T(8,128)} %get-tuple-element.148) | copy-start | bytes 1966084
  897.2 11.9 %copy-start.183 = (f32[5,1,2,1,16384]{4,0,3,2,1:T(8,128)S(1)}, f32[5,1,2,1,16384]{4,0,3,2,1:T(8,128)}, u32[]{:S(2)}) copy-start(f32[5,1,2,1,16384]{4,0,3,2,1:T(8,128)} %get-tuple-element.135) | copy-start | bytes 1966084
  897.2 13.1 %copy-start.149 = (f32[5,1,2,1,16384]{4,0,3,2,1:T(8,128)S(1)}, f32[5,1,2,1,16384]{4,0,3,2,1:T(8,128)}, u32[]{:S(2)}) copy-start(f32[5,1,2,1,16384]{4,0,3,2,1:T(8,128)} %get-tuple-element.42) | copy-start | bytes 1966084
  899.8 11.7 %copy-start.148 = (f32[5,1,2,1,16384]{4,0,3,2,1:T(8,128)S(1)}, f32[5,1,2,1,16384]{4,0,3,2,1:T(8,128)}, u32[]{:S(2)}) copy-start(f32[5,1,2,1,16384]{4,0,3,2,1:T(8,128)} %get-tuple-element.37) | copy-start | bytes 1966084
  (192 other events, 1256.9 us)
Sparse Core Ops, SparseCore 0:
  409.4 109.1 all-reduce.1
  930.4 30.4 reduce-scatter.3
where the time goes:
time: 981 us; the launch traced here: 970 us
  local copies, waits for them, and re-layouts  469 us (48%)
  other arithmetic  334 us (34%)
  waiting for transfers between devices  133 us (14%)
  between operations  17.5 us (2%)
  blocking collectives  15.3 us (2%)
    add x24, other arithmetic, product(): imag_sum = imag_sum + left_re * right_im + left_im * right_re  144 us
    slice x8, local copies, waits for them, and re-layouts, split_parts(): return [lax.index_in_dim(matrix, c, axis, keepdims=False) for c in range(8)]  143 us
    unnamed x569, local copies, waits for them, and re-layouts  114 us
    psum x1, waiting for transfers between devices, body(): lax.psum(partial_sum.astype(jnp.bfloat16), 'dir').astype(jnp.float32)  108 us
    unnamed x35, other arithmetic  101 us
    another operation x36, local copies, waits for them, and re-layouts, body(): jnp.stack(product(resid_parts, product(right_g, adjoint(model_c))), axis=3)  66.4 us
    another operation x36, local copies, waits for them, and re-layouts, body(): jnp.stack(product(adjoint(resid_parts), product(left_g, model_c)), axis=3)  54.7 us
    another operation x8, local copies, waits for them, and re-layouts, direction_gains(): right_g = jnp.tile(gain_b, (1, 1, 1, blk))[:, None]  38 us
  transfers between devices with their start and end apart: 2, of which 2 were waited for; matrix products, arithmetic and copies ran while one was open for 1% of the time, Pallas kernels for 0%

commit v1 on v0

--- a/solution.py
+++ b/solution.py
@@ -1,7 +1,14 @@
+import functools
+
 import jax
 import jax.numpy as jnp
 from jax import lax
+from jax.experimental import pallas as pl
+from jax.experimental.pallas import tpu as pltpu
 from jax.sharding import PartitionSpec as P
+
+LANES = 128
+CHUNK = 64
 
 
 def split_parts(matrix, axis):
@@ -10,33 +17,266 @@
 
 def product(left, right):
     result = [None] * 8
-    for row_index in range(2):
-        for col_index in range(2):
-            real_sum = 0.0
-            imag_sum = 0.0
-            for mid_index in range(2):
-                left_re = left[2 * row_index + mid_index]
-                left_im = left[4 + 2 * row_index + mid_index]
-                right_re = right[2 * mid_index + col_index]
-                right_im = right[4 + 2 * mid_index + col_index]
-                real_sum = real_sum + left_re * right_re - left_im * right_im
-                imag_sum = imag_sum + left_re * right_im + left_im * right_re
-            result[2 * row_index + col_index] = real_sum
-            result[4 + 2 * row_index + col_index] = imag_sum
+    for i in range(2):
+        for j in range(2):
+            re = im = None
+            for m in range(2):
+                lr, li = left[2 * i + m], left[4 + 2 * i + m]
+                rr, ri = right[2 * m + j], right[4 + 2 * m + j]
+                re_term = lr * rr - li * ri
+                im_term = lr * ri + li * rr
+                re = re_term if re is None else re + re_term
+                im = im_term if im is None else im + im_term
+            result[2 * i + j] = re
+            result[4 + 2 * i + j] = im
     return result
 
 
-def adjoint(matrix):
-    return [
-        matrix[0],
-        matrix[2],
-        matrix[1],
-        matrix[3],
-        -matrix[4],
-        -matrix[6],
-        -matrix[5],
-        -matrix[7],
-    ]
+def product_adj_right(left, right):
+    result = [None] * 8
+    for i in range(2):
+        for j in range(2):
+            re = im = None
+            for m in range(2):
+                lr, li = left[2 * i + m], left[4 + 2 * i + m]
+                rr, ri = right[2 * j + m], right[4 + 2 * j + m]
+                re_term = lr * rr + li * ri
+                im_term = li * rr - lr * ri
+                re = re_term if re is None else re + re_term
+                im = im_term if im is None else im + im_term
+            result[2 * i + j] = re
+            result[4 + 2 * i + j] = im
+    return result
+
+
+def product_adj_left(left, right):
+    result = [None] * 8
+    for i in range(2):
+        for j in range(2):
+            re = im = None
+            for m in range(2):
+                lr, li = left[2 * m + i], left[4 + 2 * m + i]
+                rr, ri = right[2 * m + j], right[4 + 2 * m + j]
+                re_term = lr * rr + li * ri
+                im_term = lr * ri - li * rr
+                re = re_term if re is None else re + re_term
+                im = im_term if im is None else im + im_term
+            result[2 * i + j] = re
+            result[4 + 2 * i + j] = im
+    return result
+
+
+def adjoint(m):
+    return [m[0], m[2], m[1], m[3], -m[4], -m[6], -m[5], -m[7]]
+
+
+def widen(src, dst, dirs):
+    for k in range(dirs):
+        for p in range(CHUNK):
+            dst[k, p * 8 : p * 8 + 8, :] = src[0, 0, k, 0, :, p * LANES : (p + 1) * LANES].astype(
+                jnp.float32
+            )
+
+
+def parts_at(ref, k, row):
+    return [ref[k, pl.ds(row + c, 8, stride=8), :] for c in range(8)]
+
+
+def forward_kernel(dirs, blocks, left_ref, right_ref, coh_ref, out_ref, wide):
+    widen(coh_ref, wide, dirs)
+
+    @pl.loop(0, CHUNK // 16)
+    def _(g):
+        halves = []
+        for h in range(2):
+            p0 = pl.multiple_of(g * 16 + h * 8, 8)
+            rows = left_ref[0, 0, pl.ds(p0, 8), :]
+            total = None
+            for k in range(dirs):
+                model = parts_at(wide, k, pl.multiple_of(p0 * 8, 64))
+                jq = [right_ref[0, 0, k * 8 + c : k * 8 + c + 1, :] for c in range(8)]
+                jp = [rows[:, k * 8 + c : k * 8 + c + 1] for c in range(8)]
+                term = product(jp, product_adj_right(model, jq))
+                total = term if total is None else [x + y for x, y in zip(total, term)]
+            halves.append(total)
+        for c in range(8):
+            both = jnp.concatenate([halves[0][c], halves[1][c]], axis=0)
+            out_ref[0, c, pl.ds(pl.multiple_of(g * 16, 16), 16), :] = both.astype(jnp.bfloat16)
+
+
+def backward_kernel(
+    dirs,
+    slot,
+    blocks,
+    counts,
+    left_ref,
+    right_ref,
+    own_ref,
+    other_ref,
+    obs_ref,
+    coh_ref,
+    res_ref,
+    first_ref,
+    second_ref,
+    wide,
+    wide_obs,
+    res,
+    acc,
+):
+    chunk = pl.program_id(1)
+    widen(coh_ref, wide, dirs)
+    for p in range(CHUNK):
+        wide_obs[0, p * 8 : p * 8 + 8, :] = obs_ref[0, 0, 0, :, p * LANES : (p + 1) * LANES].astype(
+            jnp.float32
+        )
+    used = slot < counts[0]
+    off_diag = blocks[slot, 0] < blocks[slot, 1]
+
+    @pl.loop(0, CHUNK // 16)
+    def _(g):
+        r0 = pl.multiple_of(g * 16, 16)
+        station = chunk * CHUNK + r0 + lax.broadcasted_iota(jnp.int32, (16, LANES), 0)
+        partner = lax.broadcasted_iota(jnp.int32, (16, LANES), 1)
+        upper = (jnp.where(off_diag, -1, station) < partner) & (jnp.where(used, partner, -1) >= 0)
+        for c in range(8):
+            predicted = own_ref[0, c, pl.ds(r0, 16), :].astype(jnp.float32) + other_ref[
+                0, c, pl.ds(r0, 16), :
+            ].astype(jnp.float32)
+            seen = jnp.concatenate(
+                [wide_obs[0, pl.ds((r0 + h * 8) * 8 + c, 8, stride=8), :] for h in range(2)], axis=0
+            )
+            left_over = jnp.where(upper, seen - predicted, 0.0).astype(jnp.bfloat16).astype(jnp.float32)
+            res[c, pl.ds(r0, 16), :] = left_over
+            for h in range(2):
+                wide_obs[0, pl.ds((r0 + h * 8) * 8 + c, 8, stride=8), :] = left_over[h * 8 : h * 8 + 8]
+
+    for p in range(CHUNK):
+        res_ref[0, 0, 0, :, p * LANES : (p + 1) * LANES] = wide_obs[0, p * 8 : p * 8 + 8, :].astype(
+            jnp.bfloat16
+        )
+
+    @pl.when(chunk == 0)
+    def _():
+        acc[...] = jnp.zeros_like(acc)
+
+    for k in range(dirs):
+
+        def step(g, sums, k=k):
+            p0 = pl.multiple_of(g * 8, 8)
+            model = parts_at(wide, k, pl.multiple_of(p0 * 8, 64))
+            rest = [res[c, pl.ds(p0, 8), :] for c in range(8)]
+            jq = [right_ref[0, 0, k * 8 + c : k * 8 + c + 1, :] for c in range(8)]
+            rows = left_ref[0, 0, pl.ds(p0, 8), :]
+            jp = [rows[:, k * 8 + c : k * 8 + c + 1] for c in range(8)]
+            toward_first = product_adj_right(rest, product_adj_right(model, jq))
+            for c in range(8):
+                first_ref[0, pl.ds(p0, 8), k * 8 + c : k * 8 + c + 1] = jnp.sum(
+                    toward_first[c], axis=1, keepdims=True
+                )
+            toward_second = product_adj_left(rest, product(jp, model))
+            return tuple(x + y for x, y in zip(sums, toward_second))
+
+        zero = jnp.zeros((8, LANES), jnp.float32)
+        sums = lax.fori_loop(0, CHUNK // 8, step, (zero,) * 8)
+        for c in range(8):
+            acc[k * 8 + c] += sums[c]
+
+    @pl.when(chunk == pl.num_programs(1) - 1)
+    def _():
+        second_ref[0] = jnp.sum(acc[...], axis=1)
+
+
+def fast_body(blocks, counts, gains, coherency, observed):
+    nblocks = lax.axis_size("pair")
+    dirs, chans, _, blk = gains.shape
+    maxb = blocks.shape[0]
+    base = coherency.shape[-1]
+    chunks = blk // CHUNK
+    width = CHUNK * LANES
+    comps = dirs * 8
+    whole = lax.all_gather(gains, "pair", axis=0)
+    right = jnp.transpose(whole, (0, 2, 1, 3, 4)).reshape(nblocks, chans, comps, blk)
+    left = jnp.transpose(right, (0, 1, 3, 2))
+    kind = pltpu.CompilerParams(
+        dimension_semantics=("arbitrary", "arbitrary"), vmem_limit_bytes=40 * 2**20
+    )
+    ops = 64 * dirs * chans * base
+
+    def forward(slot):
+        return pl.pallas_call(
+            functools.partial(forward_kernel, dirs),
+            grid_spec=pltpu.PrefetchScalarGridSpec(
+                num_scalar_prefetch=1,
+                grid=(chans, chunks),
+                in_specs=[
+                    pl.BlockSpec((1, 1, CHUNK, comps), lambda f, i, b: (b[slot, 0], f, i, 0)),
+                    pl.BlockSpec((1, 1, comps, blk), lambda f, i, b: (b[slot, 1], f, 0, 0)),
+                    pl.BlockSpec((1, 1, dirs, 1, 8, width), lambda f, i, b: (slot, 0, 0, f, 0, i)),
+                ],
+                out_specs=pl.BlockSpec((1, 8, CHUNK, LANES), lambda f, i, b: (f, 0, i, 0)),
+                scratch_shapes=[pltpu.VMEM((dirs, CHUNK * 8, LANES), jnp.float32)],
+            ),
+            out_shape=jax.ShapeDtypeStruct((chans, 8, blk, blk), jnp.bfloat16),
+            compiler_params=kind,
+            cost_estimate=pl.CostEstimate(
+                flops=4 * ops, bytes_accessed=dirs * chans * 8 * base * 2, transcendentals=0
+            ),
+            name="forward",
+        )(blocks, left, right, coherency)
+
+    def backward(slot, own, other):
+        return pl.pallas_call(
+            functools.partial(backward_kernel, dirs, slot),
+            grid_spec=pltpu.PrefetchScalarGridSpec(
+                num_scalar_prefetch=2,
+                grid=(chans, chunks),
+                in_specs=[
+                    pl.BlockSpec((1, 1, CHUNK, comps), lambda f, i, b, n: (b[slot, 0], f, i, 0)),
+                    pl.BlockSpec((1, 1, comps, blk), lambda f, i, b, n: (b[slot, 1], f, 0, 0)),
+                    pl.BlockSpec((1, 8, CHUNK, LANES), lambda f, i, b, n: (f, 0, i, 0)),
+                    pl.BlockSpec((1, 8, CHUNK, LANES), lambda f, i, b, n: (f, 0, i, 0)),
+                    pl.BlockSpec((1, 1, 1, 8, width), lambda f, i, b, n: (slot, 0, f, 0, i)),
+                    pl.BlockSpec((1, 1, dirs, 1, 8, width), lambda f, i, b, n: (slot, 0, 0, f, 0, i)),
+                ],
+                out_specs=[
+                    pl.BlockSpec((1, 1, 1, 8, width), lambda f, i, b, n: (0, 0, f, 0, i)),
+                    pl.BlockSpec((1, CHUNK, comps), lambda f, i, b, n: (f, i, 0)),
+                    pl.BlockSpec((1, comps, blk), lambda f, i, b, n: (f, 0, 0)),
+                ],
+                scratch_shapes=[
+                    pltpu.VMEM((dirs, CHUNK * 8, LANES), jnp.float32),
+                    pltpu.VMEM((1, CHUNK * 8, LANES), jnp.float32),
+                    pltpu.VMEM((8, CHUNK, LANES), jnp.float32),
+                    pltpu.VMEM((comps, 8, LANES), jnp.float32),
+                ],
+            ),
+            out_shape=[
+                jax.ShapeDtypeStruct((1, 1, chans, 8, base), jnp.bfloat16),
+                jax.ShapeDtypeStruct((chans, blk, comps), jnp.float32),
+                jax.ShapeDtypeStruct((chans, comps, blk), jnp.float32),
+            ],
+            compiler_params=kind,
+            cost_estimate=pl.CostEstimate(
+                flops=8 * ops, bytes_accessed=dirs * chans * 8 * base * 2, transcendentals=0
+            ),
+            name="backward",
+        )(blocks, counts, left, right, own, other, observed, coherency)
+
+    swap = [(0, 1), (1, 0)]
+    own = [forward(slot) for slot in range(maxb)]
+    other = [lax.ppermute(x, "dir", swap) for x in own]
+    pieces = [backward(slot, own[slot], other[slot]) for slot in range(maxb)]
+    residual = jnp.concatenate([p[0] for p in pieces], axis=0)
+    index = jnp.arange(nblocks)
+    gradient = jnp.zeros((nblocks, chans, comps, blk), jnp.float32)
+    for slot, (_, first, second) in enumerate(pieces):
+        on_first = (blocks[slot, 0] == index).astype(jnp.float32)[:, None, None, None]
+        on_second = (blocks[slot, 1] == index).astype(jnp.float32)[:, None, None, None]
+        gradient = gradient + on_first * jnp.swapaxes(first, 1, 2)[None] + on_second * second[None]
+    gradient = gradient.reshape(nblocks, chans, dirs, 8, blk)
+    gradient = jnp.transpose(gradient, (2, 1, 3, 0, 4)).reshape(dirs, chans, 8, nblocks * blk)
+    owned = lax.psum_scatter(gradient, ("pair", "pol"), scatter_dimension=3, tiled=True)
+    return residual, owned
 
 
 def direction_gains(one_dir, first, second, nblocks, blk):
@@ -55,7 +295,7 @@
     return keep.astype(jnp.float32)[:, None, None, None, :]
 
 
-def body(blocks, counts, gains, coherency, observed):
+def general_body(blocks, counts, gains, coherency, observed):
     nblocks = lax.axis_size("pair")
     dir_local = gains.shape[0]
     chans = gains.shape[1]
@@ -98,6 +338,13 @@
     return (residual, owned)
 
 
+def body(blocks, counts, gains, coherency, observed):
+    fits = gains.shape[3] == LANES and coherency.shape[1] == 1 and lax.axis_size("dir") == 2
+    fits = fits and lax.axis_size("pair") == 4 and blocks.shape[0] == 5
+    chosen = fast_body if fits else general_body
+    return chosen(blocks, counts, gains, coherency, observed)
+
+
 def solution(mesh):
     in_specs = (
         P(("grp", "pair"), None),

time: 981 us -> 230 us (0.23); the launches traced: 970 us -> 230 us
  local copies, waits for them, and re-layouts: 469 us -> 28 us
  other arithmetic: 334 us -> 7.25 us
  Pallas kernels: 0 us -> 131 us
  waiting for transfers between devices: 133 us -> 27.6 us
    another operation x89 -> x0, local copies, waits for them, and re-layouts: 187 us -> none  [the longest x36 66.4 us: body(): jnp.stack(product(resid_parts, product(right_g, adjoint(model_c))), axis=3)]
    slice x9 -> x1, local copies, waits for them, and re-layouts: 151 us -> 0.68 us  [fast_body(): blocks[slot, 0] == index]
    add x24 -> x1, other arithmetic: 144 us -> 1.02 us  [fast_body(): gradient + on_first * jnp.swapaxes(first, 1, 2)[None]]
    pallas_call x0 -> x10, Pallas kernels: none -> 131 us  [the longest x5 107 us: backward(): pl.pallas_call(functools.partial(backward_kernel, dirs, slot), grid_spec=...]
    psum x1 -> x0, waiting for transfers between devices: 108 us -> none  [body(): lax.psum(partial_sum.astype(jnp.bfloat16), 'dir').astype(jnp.float32)]
    unnamed x35 -> x0, other arithmetic: 101 us -> none
    unnamed x569 -> x33, local copies, waits for them, and re-layouts: 114 us -> 20.8 us
    convert_element_type x5 -> x10, other arithmetic: 36.3 us -> 6.22 us  [the longest x5 3.16 us: fast_body(): (blocks[slot, 0] == index).astype(jnp.float32)[:, None, None, None]]
  transfers between devices with their start and end apart: 2 -> 6, of which waited for: 2 -> 1; matrix products, arithmetic and copies ran while one was open for 1% -> 7% of each run, Pallas kernels for 0% -> 46%
where the time goes in v1:
time: 230 us
  Pallas kernels  131 us (57%)
  local copies, waits for them, and re-layouts  28 us (12%)
  waiting for transfers between devices  27.6 us (12%)
  blocking collectives  15.3 us (7%)
  between operations  14.9 us (6%)
  other arithmetic  7.25 us (3%)
  starting transfers between devices  5.65 us (2%)
    pallas_call x5, Pallas kernels, backward(): pl.pallas_call(functools.partial(backward_kernel, dirs, slot), grid_spec=...  107 us
    unnamed x2, waiting for transfers between devices  27.6 us
    pallas_call x5, Pallas kernels, forward(): pl.pallas_call(functools.partial(forward_kernel, dirs), grid_spec=pltpu.P...  23.6 us
    unnamed x33, local copies, waits for them, and re-layouts  20.8 us
    all_gather x1, blocking collectives, fast_body(): whole = lax.all_gather(gains, 'pair', axis=0)  15.3 us
    ppermute x5, starting transfers between devices, fast_body(): other = [lax.ppermute(x, 'dir', swap) for x in own]  5.61 us
  transfers between devices with their start and end apart: 6, of which 1 were waited for; matrix products, arithmetic and copies ran while one was open for 7% of the time, Pallas kernels for 46%

profile of v1, /device:TPU:0, one launch (start us, length us, event | category | flops | bytes accessed | tf_op | source)
XLA Modules:
  0.0 229.5 jit_solution(3095825179002509644)
XLA Ops:
  7.2 0.0 reduce-scatter.4.cloned.1.call-start
  7.2 0.8 copy.77.blocks
  8.0 15.3 %all-gather = f32[16,2,8,128]{3,2,1,0:T(8,128)S(1)} all-gather(f32[4,2,8,128]{3,2,1,0:T(8,128)} %param.7), channel_id=2, replica_groups=mesh['grp'=2,'pair'=4,'dir'=2,'pol'=2] {'pair'}, dimensions={0}, use_global_device_ids=true | all-gather | bytes 163840 | tf_op jit(solution)/shard_map/all_gather | solution.py:197
  23.3 0.2 copy.78.left_ref
  23.5 0.0 copy-start
  23.5 4.0 %copy-done = bf16[5,1,4,2,8,16384]{5,4,3,2,1,0:T(8,128)(2,1)S(1)} copy-done((bf16[5,1,4,2,8,16384]{5,4,3,2,1,0:T(8,128)(2,1)S(1)}, bf16[5,1,4,2,8,16384]{5,4,3,2,1,0:T(8,128)(2,1)}, u32[]{:S(2)}) %copy-start) | copy-done | bytes 10485784
  27.4 4.2 %forward.5.own_ref = bf16[2,8,128,128]{3,2,1,0:T(8,128)(2,1)S(1)} custom-call(s32[5,2]{1,0:T(8,128)S(1)} %copy.77.blocks, f32[4,2,128,32]{3,2,1,0:T(8,128)S(1)} %copy.78.left_ref, f32[4,2,32,128]{3,2,1,0:T(8,128)S(1)} %bitcast.163, bf16[5,1,4,2,8,16384]{5,4,3,2,1,0:T(8,128)(2,1)S(1)} %copy-done), custom_call_target="tpu_custom_call" | custom-call | flops 33554432 | bytes 2097152 | tf_op jit(solution)/shard_map/forward/pallas_call | solution.py:206
  31.7 1.6 collective-permute-start
  33.2 4.9 %forward.6.own_ref = bf16[2,8,128,128]{3,2,1,0:T(8,128)(2,1)} custom-call(s32[5,2]{1,0:T(8,128)S(1)} %copy.77.blocks, f32[4,2,128,32]{3,2,1,0:T(8,128)S(1)} %copy.78.left_ref, f32[4,2,32,128]{3,2,1,0:T(8,128)S(1)} %bitcast.164, bf16[5,1,4,2,8,16384]{5,4,3,2,1,0:T(8,128)(2,1)S(1)} %copy-done), custom_call_target="tpu_custom_call" | custom-call | flops 33554432 | bytes 2097152 | tf_op jit(solution)/shard_map/forward/pallas_call | solution.py:206
  38.1 0.5 collective-permute-start.1
  38.7 4.9 %forward.7.own_ref = bf16[2,8,128,128]{3,2,1,0:T(8,128)(2,1)} custom-call(s32[5,2]{1,0:T(8,128)S(1)} %copy.77.blocks, f32[4,2,128,32]{3,2,1,0:T(8,128)S(1)} %copy.78.left_ref, f32[4,2,32,128]{3,2,1,0:T(8,128)S(1)} %bitcast.165, bf16[5,1,4,2,8,16384]{5,4,3,2,1,0:T(8,128)(2,1)S(1)} %copy-done), custom_call_target="tpu_custom_call" | custom-call | flops 33554432 | bytes 2097152 | tf_op jit(solution)/shard_map/forward/pallas_call | solution.py:206
  43.5 1.5 collective-permute-start.2
  45.0 4.8 %forward.8.own_ref = bf16[2,8,128,128]{3,2,1,0:T(8,128)(2,1)} custom-call(s32[5,2]{1,0:T(8,128)S(1)} %copy.77.blocks, f32[4,2,128,32]{3,2,1,0:T(8,128)S(1)} %copy.78.left_ref, f32[4,2,32,128]{3,2,1,0:T(8,128)S(1)} %bitcast.166, bf16[5,1,4,2,8,16384]{5,4,3,2,1,0:T(8,128)(2,1)S(1)} %copy-done), custom_call_target="tpu_custom_call" | custom-call | flops 33554432 | bytes 2097152 | tf_op jit(solution)/shard_map/forward/pallas_call | solution.py:206
  49.8 0.5 collective-permute-start.3
  50.4 4.8 %forward.9.own_ref = bf16[2,8,128,128]{3,2,1,0:T(8,128)(2,1)} custom-call(s32[5,2]{1,0:T(8,128)S(1)} %copy.77.blocks, f32[4,2,128,32]{3,2,1,0:T(8,128)S(1)} %copy.78.left_ref, f32[4,2,32,128]{3,2,1,0:T(8,128)S(1)} %bitcast.167, bf16[5,1,4,2,8,16384]{5,4,3,2,1,0:T(8,128)(2,1)S(1)} %copy-done), custom_call_target="tpu_custom_call" | custom-call | flops 33554432 | bytes 2097152 | tf_op jit(solution)/shard_map/forward/pallas_call | solution.py:206
  55.2 1.5 collective-permute-start.4
  56.7 0.7 fusion.9
  58.0 0.6 compare_convert_fusion
  58.6 0.6 compare_convert_fusion.1
  59.3 0.7 compare_convert_fusion.2
  59.9 0.5 compare_convert_fusion.3
  60.5 0.6 compare_convert_fusion.4
  61.1 0.7 compare_convert_fusion.5
  61.8 0.6 compare_convert_fusion.6
  62.4 0.7 compare_convert_fusion.7
  63.0 0.6 compare_convert_fusion.8
  63.7 0.1 broadcast_bitcast_fusion
  63.8 0.6 broadcast_bitcast_fusion.2
  64.4 0.7 broadcast_bitcast_fusion.4
  65.1 0.6 compare_convert_fusion.9
  65.7 0.6 broadcast_bitcast_fusion.6
  66.4 0.6 broadcast_bitcast_fusion.8
  67.0 0.0 collective-permute-done.other_ref
  67.0 21.4 %backward.5 = (bf16[1,1,2,8,16384]{4,3,2,1,0:T(8,128)(2,1)S(1)}, f32[2,128,32]{2,1,0:T(8,128)S(1)}, f32[2,32,128]{2,1,0:T(8,128)S(1)}) custom-call(s32[5,2]{1,0:T(8,128)S(1)} %copy.77.blocks, s32[1]{0:T(128)S(6)} %copy.139.counts, f32[4,2,128,32]{3,2,1,0:T(8,128)S(1)} %copy.78.left_ref, f32[4,2,32,128]{3,2,1,0:T(8,128)S(1)} %bitcast.168, ...), custom_call_target="tpu_custom_call" | custom-call | flops 67108864 | bytes 2097152 | tf_op jit(solution)/shard_map/backward/pallas_call | solution.py:228
  88.4 0.8 constant_dynamic-update-slice_fusion.4
  89.2 0.7 copy.95
  89.9 0.0 collective-permute-done.1.other_ref
  89.9 21.5 %backward.6 = (bf16[1,1,2,8,16384]{4,3,2,1,0:T(8,128)(2,1)S(1)}, f32[2,128,32]{2,1,0:T(8,128)S(1)}, f32[2,32,128]{2,1,0:T(8,128)S(1)}) custom-call(s32[5,2]{1,0:T(8,128)S(1)} %copy.77.blocks, s32[1]{0:T(128)S(6)} %copy.139.counts, f32[4,2,128,32]{3,2,1,0:T(8,128)S(1)} %copy.78.left_ref, f32[4,2,32,128]{3,2,1,0:T(8,128)S(1)} %bitcast.169, ...), custom_call_target="tpu_custom_call" | custom-call | flops 67108864 | bytes 2097152 | tf_op jit(solution)/shard_map/backward/pallas_call | solution.py:228
  111.4 0.8 copy-done.2
  112.2 0.7 copy.98
  112.9 0.0 collective-permute-done.2.other_ref
  112.9 21.5 %backward.7 = (bf16[1,1,2,8,16384]{4,3,2,1,0:T(8,128)(2,1)S(1)}, f32[2,128,32]{2,1,0:T(8,128)S(1)}, f32[2,32,128]{2,1,0:T(8,128)S(1)}) custom-call(s32[5,2]{1,0:T(8,128)S(1)} %copy.77.blocks, s32[1]{0:T(128)S(6)} %copy.139.counts, f32[4,2,128,32]{3,2,1,0:T(8,128)S(1)} %copy.78.left_ref, f32[4,2,32,128]{3,2,1,0:T(8,128)S(1)} %bitcast.170, ...), custom_call_target="tpu_custom_call" | custom-call | flops 67108864 | bytes 2097152 | tf_op jit(solution)/shard_map/backward/pallas_call | solution.py:228
  134.4 0.8 copy-done.4
  135.2 0.7 copy.101
  135.9 0.0 collective-permute-done.3.other_ref
  135.9 21.5 %backward.8 = (bf16[1,1,2,8,16384]{4,3,2,1,0:T(8,128)(2,1)S(1)}, f32[2,128,32]{2,1,0:T(8,128)S(1)}, f32[2,32,128]{2,1,0:T(8,128)S(1)}) custom-call(s32[5,2]{1,0:T(8,128)S(1)} %copy.77.blocks, s32[1]{0:T(128)S(6)} %copy.139.counts, f32[4,2,128,32]{3,2,1,0:T(8,128)S(1)} %copy.78.left_ref, f32[4,2,32,128]{3,2,1,0:T(8,128)S(1)} %bitcast.171, ...), custom_call_target="tpu_custom_call" | custom-call | flops 67108864 | bytes 2097152 | tf_op jit(solution)/shard_map/backward/pallas_call | solution.py:228
  157.3 0.8 copy-done.6
  158.1 0.7 copy.104
  158.8 0.0 collective-permute-done.4.other_ref
  158.8 21.5 %backward.9 = (bf16[1,1,2,8,16384]{4,3,2,1,0:T(8,128)(2,1)S(1)}, f32[2,128,32]{2,1,0:T(8,128)S(1)}, f32[2,32,128]{2,1,0:T(8,128)S(1)}) custom-call(s32[5,2]{1,0:T(8,128)S(1)} %copy.77.blocks, s32[1]{0:T(128)S(6)} %copy.139.counts, f32[4,2,128,32]{3,2,1,0:T(8,128)S(1)} %copy.78.left_ref, f32[4,2,32,128]{3,2,1,0:T(8,128)S(1)} %bitcast.172, ...), custom_call_target="tpu_custom_call" | custom-call | flops 67108864 | bytes 2097152 | tf_op jit(solution)/shard_map/backward/pallas_call | solution.py:228
  180.3 0.8 copy-done.8
  181.1 0.6 copy-done.10
  181.7 0.1 copy.107
  181.8 1.0 fusion
  182.8 2.3 copy.110
  185.1 4.8 %reshape.111 = f32[512,64]{1,0:T(8,128)} reshape(f32[512,4,2,8]{3,2,1,0:T(2,128)} %bitcast.178) | data formatting | bytes 262144
  189.8 0.0 reduce-scatter.4.cloned.1.call-update
  189.9 0.8 constant_dynamic-update-slice_fusion.3
  190.7 0.8 constant_dynamic-update-slice_fusion.2
  191.5 0.8 constant_dynamic-update-slice_fusion.1
  192.4 0.8 constant_dynamic-update-slice_fusion
  193.2 27.6 %reduce-scatter.4.cloned.1.call-done = f32[64,64]{1,0:T(8,128)} async-done(((f32[512,64]{1,0:T(8,128)}), f32[64,64]{1,0:T(8,128)}) %reduce-scatter.4.cloned.1.call-update) | async-done | bytes 16400
  220.8 1.1 reshape.112
  221.9 0.8 copy.111
  (18 shorter events, 0.0 us)
Async XLA Ops:
  7.2 213.6 %reduce-scatter.4.cloned.1.call-start = ((), (), s32[]{:S(2)}) async-start(), calls=%async_computation.1 | async-start | bytes 294912
  23.5 4.0 %copy-start = (bf16[5,1,4,2,8,16384]{5,4,3,2,1,0:T(8,128)(2,1)S(1)}, bf16[5,1,4,2,8,16384]{5,4,3,2,1,0:T(8,128)(2,1)}, u32[]{:S(2)}) copy-start(bf16[5,1,4,2,8,16384]{5,4,3,2,1,0:T(8,128)(2,1)} %coh_ref.19) | copy-start | bytes 31457284
  31.7 35.3 %collective-permute-start = (bf16[2,8,128,128]{3,2,1,0:T(8,128)(2,1)S(1)}, bf16[2,8,128,128]{3,2,1,0:T(8,128)(2,1)S(1)}, u32[]{:S(2)}, u32[]{:S(2)}) collective-permute-start(bf16[2,8,128,128]{3,2,1,0:T(8,128)(2,1)S(1)} %forward.5.own_ref), channel_id=1, source_target_pairs={{0,2},{2,0},{1,3},{3,1},{4,6},{6,4},{5,7},{7,5},{8,10},{10,8},{9,1... | collective-permute-start | bytes 1572872 | tf_op jit(solution)/shard_map/ppermute | solution.py:267
  38.1 51.8 %collective-permute-start.1 = (bf16[2,8,128,128]{3,2,1,0:T(8,128)(2,1)}, bf16[2,8,128,128]{3,2,1,0:T(8,128)(2,1)}, u32[]{:S(2)}, u32[]{:S(2)}) collective-permute-start(bf16[2,8,128,128]{3,2,1,0:T(8,128)(2,1)} %forward.6.own_ref), channel_id=1, source_target_pairs={{0,2},{2,0},{1,3},{3,1},{4,6},{6,4},{5,7},{7,5},{8,10},{10,8},{9,1... | collective-permute-start | bytes 1572872 | tf_op jit(solution)/shard_map/ppermute | solution.py:267
  43.5 69.4 %collective-permute-start.2 = (bf16[2,8,128,128]{3,2,1,0:T(8,128)(2,1)}, bf16[2,8,128,128]{3,2,1,0:T(8,128)(2,1)}, u32[]{:S(2)}, u32[]{:S(2)}) collective-permute-start(bf16[2,8,128,128]{3,2,1,0:T(8,128)(2,1)} %forward.7.own_ref), channel_id=1, source_target_pairs={{0,2},{2,0},{1,3},{3,1},{4,6},{6,4},{5,7},{7,5},{8,10},{10,8},{9,1... | collective-permute-start | bytes 1572872 | tf_op jit(solution)/shard_map/ppermute | solution.py:267
  49.8 6.9 %copy-start.11 = (s32[5,2]{0,1:T(2,128)S(1)}, s32[5,2]{0,1:T(2,128)}, u32[]{:S(2)}) copy-start(s32[5,2]{0,1:T(2,128)} %param.5) | copy-start | bytes 124
  49.8 17.2 %copy-start.1 = (bf16[5,1,2,8,16384]{4,3,2,1,0:T(8,128)(2,1)S(1)}, bf16[5,1,2,8,16384]{4,3,2,1,0:T(8,128)(2,1)}, u32[]{:S(2)}) copy-start(bf16[5,1,2,8,16384]{4,3,2,1,0:T(8,128)(2,1)} %obs_ref.9) | copy-start | bytes 7864324
  49.8 86.0 %collective-permute-start.3 = (bf16[2,8,128,128]{3,2,1,0:T(8,128)(2,1)}, bf16[2,8,128,128]{3,2,1,0:T(8,128)(2,1)}, u32[]{:S(2)}, u32[]{:S(2)}) collective-permute-start(bf16[2,8,128,128]{3,2,1,0:T(8,128)(2,1)} %forward.8.own_ref), channel_id=1, source_target_pairs={{0,2},{2,0},{1,3},{3,1},{4,6},{6,4},{5,7},{7,5},{8,10},{10,8},{9,1... | collective-permute-start | bytes 1572872 | tf_op jit(solution)/shard_map/ppermute | solution.py:267
  55.2 103.6 %collective-permute-start.4 = (bf16[2,8,128,128]{3,2,1,0:T(8,128)(2,1)}, bf16[2,8,128,128]{3,2,1,0:T(8,128)(2,1)}, u32[]{:S(2)}, u32[]{:S(2)}) collective-permute-start(bf16[2,8,128,128]{3,2,1,0:T(8,128)(2,1)} %forward.9.own_ref), channel_id=1, source_target_pairs={{0,2},{2,0},{1,3},{3,1},{4,6},{6,4},{5,7},{7,5},{8,10},{10,8},{9,1... | collective-permute-start | bytes 1572872 | tf_op jit(solution)/shard_map/ppermute | solution.py:267
  111.4 0.8 copy-start.2
  134.4 0.8 copy-start.4
  157.3 0.8 copy-start.6
  180.3 0.8 copy-start.8
  181.1 0.6 copy-start.10
  181.8 8.1 %copy-start.3 = (bf16[1,1,2,8,16384]{4,3,2,1,0:T(8,128)(2,1)S(1)}, bf16[1,1,2,8,16384]{4,3,2,1,0:T(8,128)(2,1)}, u32[]{:S(2)}) copy-start(bf16[1,1,2,8,16384]{4,3,2,1,0:T(8,128)(2,1)} %copy-done.2) | copy-start | bytes 1572868
  182.8 7.9 %copy-start.5 = (bf16[1,1,2,8,16384]{4,3,2,1,0:T(8,128)(2,1)S(1)}, bf16[1,1,2,8,16384]{4,3,2,1,0:T(8,128)(2,1)}, u32[]{:S(2)}) copy-start(bf16[1,1,2,8,16384]{4,3,2,1,0:T(8,128)(2,1)} %copy-done.4) | copy-start | bytes 1572868
  185.1 6.5 %copy-start.7 = (bf16[1,1,2,8,16384]{4,3,2,1,0:T(8,128)(2,1)S(1)}, bf16[1,1,2,8,16384]{4,3,2,1,0:T(8,128)(2,1)}, u32[]{:S(2)}) copy-start(bf16[1,1,2,8,16384]{4,3,2,1,0:T(8,128)(2,1)} %copy-done.6) | copy-start | bytes 1572868
  185.1 7.3 %copy-start.9 = (bf16[1,1,2,8,16384]{4,3,2,1,0:T(8,128)(2,1)S(1)}, bf16[1,1,2,8,16384]{4,3,2,1,0:T(8,128)(2,1)}, u32[]{:S(2)}) copy-start(bf16[1,1,2,8,16384]{4,3,2,1,0:T(8,128)(2,1)} %copy-done.8) | copy-start | bytes 1572868
Sparse Core Ops, SparseCore 0:
  190.0 30.7 reduce-scatter.3

commit v2 on v1

v2 whole, which is shorter than its diff:
```python
import functools

import jax
import jax.numpy as jnp
from jax import lax
from jax.experimental import pallas as pl
from jax.experimental.pallas import tpu as pltpu
from jax.sharding import PartitionSpec as P

LANES = 128


def split_parts(matrix, axis):
    return [lax.index_in_dim(matrix, c, axis, keepdims=False) for c in range(8)]


def product(left, right):
    result = [None] * 8
    for i in range(2):
        for j in range(2):
            re = im = None
            for m in range(2):
                lr, li = left[2 * i + m], left[4 + 2 * i + m]
                rr, ri = right[2 * m + j], right[4 + 2 * m + j]
                re_term = lr * rr - li * ri
                im_term = lr * ri + li * rr
                re = re_term if re is None else re + re_term
                im = im_term if im is None else im + im_term
            result[2 * i + j] = re
            result[4 + 2 * i + j] = im
    return result


def product_adj_right(left, right):
    result = [None] * 8
    for i in range(2):
        for j in range(2):
            re = im = None
            for m in range(2):
                lr, li = left[2 * i + m], left[4 + 2 * i + m]
                rr, ri = right[2 * j + m], right[4 + 2 * j + m]
                re_term = lr * rr + li * ri
                im_term = li * rr - lr * ri
                re = re_term if re is None else re + re_term
                im = im_term if im is None else im + im_term
            result[2 * i + j] = re
            result[4 + 2 * i + j] = im
    return result


def product_adj_left(left, right):
    result = [None] * 8
    for i in range(2):
        for j in range(2):
            re = im = None
            for m in range(2):
                lr, li = left[2 * m + i], left[4 + 2 * m + i]
                rr, ri = right[2 * m + j], right[4 + 2 * m + j]
                re_term = lr * rr + li * ri
                im_term = lr * ri - li * rr
                re = re_term if re is None else re + re_term
                im = im_term if im is None else im + im_term
            result[2 * i + j] = re
            result[4 + 2 * i + j] = im
    return result


def adjoint(m):
    return [m[0], m[2], m[1], m[3], -m[4], -m[6], -m[5], -m[7]]


MESH = pl.DeviceIdType.MESH


def widen(tile, dst, base):
    for p in range(16):
        dst[base + p * 8 : base + p * 8 + 8, :] = tile(p).astype(jnp.float32)


def parts_at(ref, row):
    return [ref[pl.ds(row + c, 8, stride=8), :] for c in range(8)]


def gather_kernel(nblocks, gains, left, right, land, send_sem, recv_sem):
    dirs, chans, _, blk = gains.shape
    me = lax.axis_index("pair")
    barrier = pltpu.get_barrier_semaphore()
    others = [lax.rem(me + d, nblocks) for d in range(1, nblocks)]
    for other in others:
        pl.semaphore_signal(barrier, inc=1, device_id={"pair": other}, device_id_type=MESH)
    pl.semaphore_wait(barrier, nblocks - 1)
    copies = []
    for d, other in enumerate(others):
        copy = pltpu.make_async_remote_copy(
            src_ref=gains,
            dst_ref=land.at[d],
            send_sem=send_sem.at[d],
            recv_sem=recv_sem.at[d],
            device_id={"pair": other},
            device_id_type=MESH,
        )
        copy.start()
        copies.append(copy)
    pad = jnp.zeros((LANES - dirs * 8, LANES), jnp.float32)
    for d in range(nblocks):
        owner = me if d == 0 else lax.rem(me + nblocks - d, nblocks)
        if d > 0:
            copies[d - 1].wait_recv()
        for f in range(chans):
            tiles = [gains[k, f] if d == 0 else land[d - 1, k, f] for k in range(dirs)]
            table = jnp.concatenate(tiles, axis=0)
            right[owner, f] = table
            left[owner, f] = jnp.transpose(jnp.concatenate([table, pad], axis=0))[:, : dirs * 8]
    for copy in copies:
        copy.wait_send()


def reduce_kernel(nblocks, npol, weights, *refs):
    maxb = weights.shape[1]
    firsts, seconds = refs[:maxb], refs[maxb : 2 * maxb]
    out, outgoing, land, send_sem, recv_sem = refs[2 * maxb :]
    dirs = out.shape[0]
    me, pol = lax.axis_index("pair"), lax.axis_index("pol")
    barrier = pltpu.get_barrier_semaphore()
    peers = []
    for dz in range(nblocks):
        for dp in range(npol):
            if dz or dp:
                peers.append((lax.rem(me + dz, nblocks), lax.rem(pol + dp, npol)))
    for z, q in peers:
        pl.semaphore_signal(barrier, inc=1, device_id={"pair": z, "pol": q}, device_id_type=MESH)
    half = LANES // 2
    lower = lax.broadcasted_iota(jnp.int32, (dirs * 8, LANES), 1) < half
    for n in range(nblocks):
        sums = []
        for f in range(2):
            total = None
            for s in range(maxb):
                term = weights[0, s, n] * firsts[s][f] + weights[1, s, n] * seconds[s][f]
                total = term if total is None else total + term
            sums.append(total)
        outgoing[n, 0] = jnp.where(lower, sums[0], pltpu.roll(sums[1], half, 1))
        outgoing[n, 1] = jnp.where(lower, pltpu.roll(sums[0], half, 1), sums[1])
    pl.semaphore_wait(barrier, len(peers))
    copies = []
    for i, (z, q) in enumerate(peers):
        copy = pltpu.make_async_remote_copy(
            src_ref=outgoing.at[z, q],
            dst_ref=land.at[i],
            send_sem=send_sem.at[i],
            recv_sem=recv_sem.at[i],
            device_id={"pair": z, "pol": q},
            device_id_type=MESH,
        )
        copy.start()
        copies.append(copy)
    total = outgoing[me, pol]
    for i, copy in enumerate(copies):
        copy.wait_recv()
        total = total + land[i]
    for k in range(dirs):
        for f in range(2):
            out[k, f] = total[k * 8 : k * 8 + 8, f * half : f * half + half]
    for copy in copies:
        copy.wait_send()


def forward_kernel(dirs, blocks, left_ref, right_ref, coh_ref, out_ref, wide):
    blk = left_ref.shape[2]

    @pl.loop(0, blk // 16)
    def _(g):
        p0 = pl.multiple_of(g * 16, 16)
        for k in range(dirs):
            widen(
                lambda p, k=k: coh_ref[0, 0, k, 0, :, pl.ds(pl.multiple_of((p0 + p) * LANES, LANES), LANES)],
                wide,
                k * 128,
            )
        halves = []
        for h in range(2):
            rows = left_ref[0, 0, pl.ds(p0 + h * 8, 8), :]
            total = None
            for k in range(dirs):
                model = parts_at(wide, k * 128 + h * 64)
                jq = [right_ref[0, 0, k * 8 + c : k * 8 + c + 1, :] for c in range(8)]
                jp = [rows[:, k * 8 + c : k * 8 + c + 1] for c in range(8)]
                term = product(jp, product_adj_right(model, jq))
                total = term if total is None else [x + y for x, y in zip(total, term)]
            halves.append(total)
        for c in range(8):
            both = jnp.concatenate([halves[0][c], halves[1][c]], axis=0)
            out_ref[0, c, pl.ds(p0, 16), :] = both.astype(jnp.bfloat16)


def backward_kernel(
    dirs,
    slot,
    blocks,
    counts,
    left_ref,
    right_ref,
    own_ref,
    other_ref,
    obs_ref,
    coh_ref,
    *refs,
):
    res_ref, first_ref, second_ref, wide, wide_obs, acc, sums_first = refs[-7:]
    blk = left_ref.shape[2]
    used = slot < counts[0]
    off_diag = blocks[slot, 0] < blocks[slot, 1]
    acc[...] = jnp.zeros_like(acc)

    @pl.loop(0, blk // 16)
    def _(g):
        p0 = pl.multiple_of(g * 16, 16)

        def lanes(p):
            return pl.ds(pl.multiple_of((p0 + p) * LANES, LANES), LANES)

        widen(lambda p: obs_ref[0, 0, 0, :, lanes(p)], wide_obs, 0)
        for k in range(dirs):
            widen(lambda p, k=k: coh_ref[0, 0, k, 0, :, lanes(p)], wide, k * 128)
        station = p0 + lax.broadcasted_iota(jnp.int32, (16, LANES), 0)
        partner = lax.broadcasted_iota(jnp.int32, (16, LANES), 1)
        keep = (jnp.where(off_diag, -1, station) < partner) & (jnp.where(used, partner, -1) >= 0)
        rest = []
        for c in range(8):
            predicted = own_ref[0, c, pl.ds(p0, 16), :].astype(jnp.float32) + other_ref[
                0, c, pl.ds(p0, 16), :
            ].astype(jnp.float32)
            seen = jnp.concatenate(
                [wide_obs[pl.ds(h * 64 + c, 8, stride=8), :] for h in range(2)], axis=0
            )
            left_over = jnp.where(keep, seen - predicted, 0.0).astype(jnp.bfloat16).astype(jnp.float32)
            rest.append(left_over)
            for h in range(2):
                wide_obs[pl.ds(h * 64 + c, 8, stride=8), :] = left_over[h * 8 : h * 8 + 8]
        for p in range(16):
            res_ref[0, 0, 0, :, lanes(p)] = wide_obs[p * 8 : p * 8 + 8, :].astype(jnp.bfloat16)
        for k in range(dirs):
            total = None
            for h in range(2):
                model = parts_at(wide, k * 128 + h * 64)
                resid = [r[h * 8 : h * 8 + 8] for r in rest]
                jq = [right_ref[0, 0, k * 8 + c : k * 8 + c + 1, :] for c in range(8)]
                rows = left_ref[0, 0, pl.ds(p0 + h * 8, 8), :]
                jp = [rows[:, k * 8 + c : k * 8 + c + 1] for c in range(8)]
                toward_first = product_adj_right(resid, product_adj_right(model, jq))
                for c in range(8):
                    sums_first[pl.ds(p0 + h * 8, 8), k * 8 + c : k * 8 + c + 1] = jnp.sum(
                        toward_first[c], axis=1, keepdims=True
                    )
                toward_second = product_adj_left(resid, product(jp, model))
                total = toward_second if h == 0 else [x + y for x, y in zip(total, toward_second)]
            for c in range(8):
                acc[k * 8 + c] += total[c]

    second_ref[0] = jnp.sum(acc[...], axis=1)
    first_ref[0] = jnp.transpose(sums_first[...])[: dirs * 8]


def fast_body(blocks, counts, gains, coherency, observed):
    nblocks = lax.axis_size("pair")
    npol = lax.axis_size("pol")
    dirs, chans, _, blk = gains.shape
    maxb = blocks.shape[0]
    base = coherency.shape[-1]
    comps = dirs * 8
    vmem = pl.BlockSpec(memory_space=pltpu.VMEM)
    left, right = pl.pallas_call(
        functools.partial(gather_kernel, nblocks),
        out_shape=[
            jax.ShapeDtypeStruct((nblocks, chans, blk, comps), jnp.float32),
            jax.ShapeDtypeStruct((nblocks, chans, comps, blk), jnp.float32),
        ],
        in_specs=[vmem],
        out_specs=[vmem, vmem],
        scratch_shapes=[
            pltpu.VMEM((nblocks - 1,) + gains.shape, jnp.float32),
            pltpu.SemaphoreType.DMA((nblocks - 1,)),
            pltpu.SemaphoreType.DMA((nblocks - 1,)),
        ],
        compiler_params=pltpu.CompilerParams(
            collective_id=0, has_side_effects=True, vmem_limit_bytes=16 * 2**20
        ),
        name="gather_gains",
    )(gains)
    kind = pltpu.CompilerParams(dimension_semantics=("arbitrary",), vmem_limit_bytes=24 * 2**20)
    ops = 64 * dirs * chans * base

    def forward(slot):
        return pl.pallas_call(
            functools.partial(forward_kernel, dirs),
            grid_spec=pltpu.PrefetchScalarGridSpec(
                num_scalar_prefetch=1,
                grid=(chans,),
                in_specs=[
                    pl.BlockSpec((1, 1, blk, comps), lambda f, b: (b[slot, 0], f, 0, 0)),
                    pl.BlockSpec((1, 1, comps, blk), lambda f, b: (b[slot, 1], f, 0, 0)),
                    pl.BlockSpec((1, 1, dirs, 1, 8, base), lambda f, b: (slot, 0, 0, f, 0, 0)),
                ],
                out_specs=pl.BlockSpec((1, 8, blk, LANES), lambda f, b: (f, 0, 0, 0)),
                scratch_shapes=[pltpu.VMEM((dirs * 128, LANES), jnp.float32)],
            ),
            out_shape=jax.ShapeDtypeStruct((chans, 8, blk, blk), jnp.bfloat16),
            compiler_params=kind,
            cost_estimate=pl.CostEstimate(
                flops=4 * ops, bytes_accessed=dirs * chans * 8 * base * 2, transcendentals=0
            ),
            name="forward",
        )(blocks, left, right, coherency)

    def backward(slot, own, other, residual):
        held = [] if residual is None else [residual]
        return pl.pallas_call(
            functools.partial(backward_kernel, dirs, slot),
            grid_spec=pltpu.PrefetchScalarGridSpec(
                num_scalar_prefetch=2,
                grid=(chans,),
                in_specs=[
                    pl.BlockSpec((1, 1, blk, comps), lambda f, b, n: (b[slot, 0], f, 0, 0)),
                    pl.BlockSpec((1, 1, comps, blk), lambda f, b, n: (b[slot, 1], f, 0, 0)),
                    pl.BlockSpec((1, 8, blk, LANES), lambda f, b, n: (f, 0, 0, 0)),
                    pl.BlockSpec((1, 8, blk, LANES), lambda f, b, n: (f, 0, 0, 0)),
                    pl.BlockSpec((1, 1, 1, 8, base), lambda f, b, n: (slot, 0, f, 0, 0)),
                    pl.BlockSpec((1, 1, dirs, 1, 8, base), lambda f, b, n: (slot, 0, 0, f, 0, 0)),
                ]
                + [pl.BlockSpec(memory_space=pl.ANY)] * len(held),
                out_specs=[
                    pl.BlockSpec((1, 1, 1, 8, base), lambda f, b, n: (slot, 0, f, 0, 0)),
                    pl.BlockSpec((1, comps, blk), lambda f, b, n: (f, 0, 0)),
                    pl.BlockSpec((1, comps, blk), lambda f, b, n: (f, 0, 0)),
                ],
                scratch_shapes=[
                    pltpu.VMEM((dirs * 128, LANES), jnp.float32),
                    pltpu.VMEM((128, LANES), jnp.float32),
                    pltpu.VMEM((comps, 8, LANES), jnp.float32),
                    pltpu.VMEM((blk, LANES), jnp.float32),
                ],
            ),
            out_shape=[
                jax.ShapeDtypeStruct(observed.shape, jnp.bfloat16),
                jax.ShapeDtypeStruct((chans, comps, blk), jnp.float32),
                jax.ShapeDtypeStruct((chans, comps, blk), jnp.float32),
            ],
            input_output_aliases={8: 0} if held else {},
            compiler_params=kind,
            cost_estimate=pl.CostEstimate(
                flops=8 * ops, bytes_accessed=dirs * chans * 8 * base * 2, transcendentals=0
            ),
            name="backward",
        )(blocks, counts, left, right, own, other, observed, coherency, *held)

    swap = [(0, 1), (1, 0)]
    own = [forward(slot) for slot in range(maxb)]
    other = [lax.ppermute(x, "dir", swap) for x in own]
    residual = None
    firsts, seconds = [], []
    for slot in range(maxb):
        residual, first, second = backward(slot, own[slot], other[slot], residual)
        firsts.append(first)
        seconds.append(second)
    index = jnp.arange(nblocks)
    weights = (blocks.T[:, :, None] == index[None, None, :]).astype(jnp.float32)
    peers = nblocks * npol - 1
    owned = pl.pallas_call(
        functools.partial(reduce_kernel, nblocks, npol),
        out_shape=jax.ShapeDtypeStruct((dirs, chans, 8, blk // npol), jnp.float32),
        in_specs=[pl.BlockSpec(memory_space=pltpu.SMEM)] + [vmem] * (2 * maxb),
        out_specs=vmem,
        scratch_shapes=[
            pltpu.VMEM((nblocks, npol, comps, LANES), jnp.float32),
            pltpu.VMEM((peers, comps, LANES), jnp.float32),
            pltpu.SemaphoreType.DMA((peers,)),
            pltpu.SemaphoreType.DMA((peers,)),
        ],
        compiler_params=pltpu.CompilerParams(
            collective_id=1, has_side_effects=True, vmem_limit_bytes=16 * 2**20
        ),
        name="reduce_gradient",
    )(weights, *firsts, *seconds)
    return residual, owned


def direction_gains(one_dir, first, second, nblocks, blk):
    table = one_dir.reshape(one_dir.shape[0], 8, nblocks, blk)
    gain_a = jnp.moveaxis(jnp.take(table, first, axis=2), 2, 0)
    gain_b = jnp.moveaxis(jnp.take(table, second, axis=2), 2, 0)
    left_g = jnp.repeat(gain_a, blk, axis=3)[:, None]
    right_g = jnp.tile(gain_b, (1, 1, 1, blk))[:, None]
    return (split_parts(left_g, 3), split_parts(right_g, 3))


def baseline_mask(first, second, used, blk):
    pair_index = jnp.arange(blk * blk)
    upper = pair_index // blk < pair_index % blk
    keep = used[:, None] & ((first < second)[:, None] | upper[None, :])
    return keep.astype(jnp.float32)[:, None, None, None, :]


def general_body(blocks, counts, gains, coherency, observed):
    nblocks = lax.axis_size("pair")
    dir_local = gains.shape[0]
    chans = gains.shape[1]
    blk = gains.shape[3]
    maxb = blocks.shape[0]
    whole = lax.all_gather(gains, "pair", axis=3, tiled=True)
    first = blocks[:, 0]
    second = blocks[:, 1]
    used = jnp.arange(maxb) < counts[0]
    mask = baseline_mask(first, second, used, blk)
    partial_sum = jnp.zeros(observed.shape, jnp.float32)
    for local in range(dir_local):
        left_g, right_g = direction_gains(whole[local], first, second, nblocks, blk)
        model_c = split_parts(coherency[:, :, local].astype(jnp.float32), 3)
        partial_sum = partial_sum + jnp.stack(
            product(product(left_g, model_c), adjoint(right_g)), axis=3
        )
    predicted = lax.psum(partial_sum.astype(jnp.bfloat16), "dir").astype(jnp.float32)
    residual = (mask * (observed.astype(jnp.float32) - predicted)).astype(jnp.bfloat16)
    resid_parts = split_parts(residual.astype(jnp.float32), 3)
    onehot_first = (first[:, None] == jnp.arange(nblocks)[None, :]).astype(jnp.float32)
    onehot_second = (second[:, None] == jnp.arange(nblocks)[None, :]).astype(jnp.float32)
    grads = []
    for local in range(dir_local):
        left_g, right_g = direction_gains(whole[local], first, second, nblocks, blk)
        model_c = split_parts(coherency[:, :, local].astype(jnp.float32), 3)
        toward_first = jnp.stack(product(resid_parts, product(right_g, adjoint(model_c))), axis=3)
        toward_second = jnp.stack(product(adjoint(resid_parts), product(left_g, model_c)), axis=3)
        toward_first = jnp.sum(toward_first, axis=1).reshape(maxb, chans, 8, blk, blk).sum(axis=4)
        toward_second = jnp.sum(toward_second, axis=1).reshape(maxb, chans, 8, blk, blk).sum(axis=3)
        grad_dir = jnp.einsum(
            "scxb,sn->cxnb", toward_first, onehot_first, precision=lax.Precision.HIGHEST
        )
        grad_dir = grad_dir + jnp.einsum(
            "scxb,sn->cxnb", toward_second, onehot_second, precision=lax.Precision.HIGHEST
        )
        grads.append(grad_dir.reshape(chans, 8, nblocks * blk))
    gradient = jnp.stack(grads, axis=0)
    owned = lax.psum_scatter(gradient, ("pair", "pol"), scatter_dimension=3, tiled=True)
    return (residual, owned)


def body(blocks, counts, gains, coherency, observed):
    fits = gains.shape[3] == LANES and coherency.shape[1] == 1 and lax.axis_size("dir") == 2
    fits = fits and gains.shape[1] == 2 and lax.axis_size("pol") == 2 and lax.axis_size("pair") <= 8
    chosen = fast_body if fits else general_body
    return chosen(blocks, counts, gains, coherency, observed)


def solution(mesh):
    in_specs = (
        P(("grp", "pair"), None),
        P(("grp", "pair")),
        P(("grp", "dir"), None, None, "pair"),
        P(("grp", "pair"), "pol", "dir", None, None, None),
        P(("grp", "pair"), "pol", None, None, None),
    )
    out_specs = (
        P(("grp", "pair"), "pol", None, None, None),
        P(("grp", "dir"), None, None, ("pair", "pol")),
    )
    return jax.shard_map(body, mesh=mesh, in_specs=in_specs, out_specs=out_specs, check_vma=False)
```

time: 230 us -> 103 us (0.45)
  Pallas kernels: 131 us -> 89.5 us
  waiting for transfers between devices: 27.6 us -> 0.01 us
  local copies, waits for them, and re-layouts: 28 us -> 6.13 us
  blocking collectives: 15.3 us -> 0 us
  between operations: 14.9 us -> 1.38 us
  other arithmetic: 7.25 us -> 0.07 us
    pallas_call x5, Pallas kernels: 107 us -> 53.2 us  [backward(): pl.pallas_call(functools.partial(backward_kernel, dirs, slot), grid_spec=...]
    unnamed x2 -> x0, waiting for transfers between devices: 27.6 us -> none
    pallas_call x0 -> x2, Pallas kernels: none -> 16.4 us  [the longest x1 8.62 us: fast_body(): pl.pallas_call(functools.partial(gather_kernel, nblocks), out_shape=[jax....]
    all_gather x1 -> x0, blocking collectives: 15.3 us -> none  [fast_body(): whole = lax.all_gather(gains, 'pair', axis=0)]
    unnamed x33 -> x10, local copies, waits for them, and re-layouts: 20.8 us -> 6.13 us
    convert_element_type x10 -> x1, other arithmetic: 6.22 us -> 0.07 us  [fast_body(): weights = (blocks.T[:, :, None] == index[None, None, :]).astype(jnp.float32)]
    pallas_call x5, Pallas kernels: 23.6 us -> 19.8 us  [forward(): pl.pallas_call(functools.partial(forward_kernel, dirs), grid_spec=pltpu.P...]
    transpose x6 -> x0, local copies, waits for them, and re-layouts: 3.01 us -> none  [the longest x5 2.81 us: fast_body(): jnp.swapaxes(first, 1, 2)[None]]
  transfers between devices with their start and end apart: 6 -> 5, of which waited for: 1 -> 0; matrix products, arithmetic and copies ran while one was open for 7% -> 0% of each run, Pallas kernels for 46% -> 57%
where the time goes in v2:
time: 103 us
  Pallas kernels  89.5 us (87%)
  local copies, waits for them, and re-layouts  6.13 us (6%)
  starting transfers between devices  5.87 us (6%)
  between operations  1.38 us (1%)
    pallas_call x5, Pallas kernels, backward(): pl.pallas_call(functools.partial(backward_kernel, dirs, slot), grid_spec=...  53.2 us
    pallas_call x5, Pallas kernels, forward(): pl.pallas_call(functools.partial(forward_kernel, dirs), grid_spec=pltpu.P...  19.8 us
    pallas_call x1, Pallas kernels, fast_body(): pl.pallas_call(functools.partial(gather_kernel, nblocks), out_shape=[jax....  8.62 us
    pallas_call x1, Pallas kernels, fast_body(): pl.pallas_call(functools.partial(reduce_kernel, nblocks, npol), out_shape...  7.83 us
    unnamed x10, local copies, waits for them, and re-layouts  6.13 us
    ppermute x5, starting transfers between devices, fast_body(): other = [lax.ppermute(x, 'dir', swap) for x in own]  5.87 us
  transfers between devices with their start and end apart: 5, of which 0 were waited for; matrix products, arithmetic and copies ran while one was open for 0% of the time, Pallas kernels for 57%

profile of v2, /device:TPU:0, one launch (start us, length us, event | category | flops | bytes accessed | tf_op | source)
XLA Modules:
  0.0 102.9 jit_solution(6442905199668316433)
XLA Ops:
  0.6 0.0 copy-start.2
  0.6 0.7 copy-done.2
  1.4 8.6 %gather_gains.1 = (f32[4,2,128,32]{3,2,1,0:T(8,128)S(1)}, f32[4,2,32,128]{3,2,1,0:T(8,128)S(1)}) custom-call(f32[4,2,8,128]{3,2,1,0:T(8,128)S(1)} %copy-done.2), custom_call_target="tpu_custom_call" | custom-call | tf_op jit(solution)/shard_map/gather_gains/pallas_call | solution.py:272
  10.0 0.8 copy.20.blocks
  10.8 0.0 copy-start
  10.8 4.0 %copy-done = bf16[5,1,4,2,8,16384]{5,4,3,2,1,0:T(8,128)(2,1)S(1)} copy-done((bf16[5,1,4,2,8,16384]{5,4,3,2,1,0:T(8,128)(2,1)S(1)}, bf16[5,1,4,2,8,16384]{5,4,3,2,1,0:T(8,128)(2,1)}, u32[]{:S(2)}) %copy-start) | copy-done | bytes 10485784
  14.8 4.0 %forward.9.own_ref = bf16[2,8,128,128]{3,2,1,0:T(8,128)(2,1)S(1)} custom-call(s32[5,2]{1,0:T(8,128)S(1)} %copy.20.blocks, f32[4,2,128,32]{3,2,1,0:T(8,128)S(1)} %get-tuple-element.19.left_ref, f32[4,2,32,128]{3,2,1,0:T(8,128)S(1)} %get-tuple-element.20.right_ref, bf16[5,1,4,2,8,16384]{5,4,3,2,1,0:T(8,128)(2,1)S(1)} %copy-done), custom_call_target="tpu_custom_call" | custom-call | flops 33554432 | bytes 2097152 | tf_op jit(solution)/shard_map/forward/pallas_call | solution.py:294
  18.7 1.6 %collective-permute-start.4 = (bf16[2,8,128,128]{3,2,1,0:T(8,128)(2,1)S(1)}, bf16[2,8,128,128]{3,2,1,0:T(8,128)(2,1)S(1)}, u32[]{:S(2)}, u32[]{:S(2)}) collective-permute-start(bf16[2,8,128,128]{3,2,1,0:T(8,128)(2,1)S(1)} %forward.9.own_ref), channel_id=1, source_target_pairs={{0,2},{2,0},{1,3},{3,1},{4,6},{6,4},{5,7},{7,5},{8,10},{10,8},{9,1... | collective-permute-start | bytes 1572872 | tf_op jit(solution)/shard_map/ppermute | solution.py:358
  20.3 4.0 %forward.8.own_ref = bf16[2,8,128,128]{3,2,1,0:T(8,128)(2,1)S(1)} custom-call(s32[5,2]{1,0:T(8,128)S(1)} %copy.20.blocks, f32[4,2,128,32]{3,2,1,0:T(8,128)S(1)} %get-tuple-element.19.left_ref, f32[4,2,32,128]{3,2,1,0:T(8,128)S(1)} %get-tuple-element.20.right_ref, bf16[5,1,4,2,8,16384]{5,4,3,2,1,0:T(8,128)(2,1)S(1)} %copy-done), custom_call_target="tpu_custom_call" | custom-call | flops 33554432 | bytes 2097152 | tf_op jit(solution)/shard_map/forward/pallas_call | solution.py:294
  24.3 0.6 collective-permute-start.3
  24.9 4.0 %forward.7.own_ref = bf16[2,8,128,128]{3,2,1,0:T(8,128)(2,1)S(1)} custom-call(s32[5,2]{1,0:T(8,128)S(1)} %copy.20.blocks, f32[4,2,128,32]{3,2,1,0:T(8,128)S(1)} %get-tuple-element.19.left_ref, f32[4,2,32,128]{3,2,1,0:T(8,128)S(1)} %get-tuple-element.20.right_ref, bf16[5,1,4,2,8,16384]{5,4,3,2,1,0:T(8,128)(2,1)S(1)} %copy-done), custom_call_target="tpu_custom_call" | custom-call | flops 33554432 | bytes 2097152 | tf_op jit(solution)/shard_map/forward/pallas_call | solution.py:294
  28.8 1.6 %collective-permute-start.2 = (bf16[2,8,128,128]{3,2,1,0:T(8,128)(2,1)S(1)}, bf16[2,8,128,128]{3,2,1,0:T(8,128)(2,1)S(1)}, u32[]{:S(2)}, u32[]{:S(2)}) collective-permute-start(bf16[2,8,128,128]{3,2,1,0:T(8,128)(2,1)S(1)} %forward.7.own_ref), channel_id=1, source_target_pairs={{0,2},{2,0},{1,3},{3,1},{4,6},{6,4},{5,7},{7,5},{8,10},{10,8},{9,1... | collective-permute-start | bytes 1572872 | tf_op jit(solution)/shard_map/ppermute | solution.py:358
  30.4 4.0 %forward.6.own_ref = bf16[2,8,128,128]{3,2,1,0:T(8,128)(2,1)S(1)} custom-call(s32[5,2]{1,0:T(8,128)S(1)} %copy.20.blocks, f32[4,2,128,32]{3,2,1,0:T(8,128)S(1)} %get-tuple-element.19.left_ref, f32[4,2,32,128]{3,2,1,0:T(8,128)S(1)} %get-tuple-element.20.right_ref, bf16[5,1,4,2,8,16384]{5,4,3,2,1,0:T(8,128)(2,1)S(1)} %copy-done), custom_call_target="tpu_custom_call" | custom-call | flops 33554432 | bytes 2097152 | tf_op jit(solution)/shard_map/forward/pallas_call | solution.py:294
  34.3 0.0 copy-start.3
  34.4 0.0 copy-start.1
  34.4 0.6 collective-permute-start.1
  35.0 4.0 %forward.5.own_ref = bf16[2,8,128,128]{3,2,1,0:T(8,128)(2,1)S(1)} custom-call(s32[5,2]{1,0:T(8,128)S(1)} %copy.20.blocks, f32[4,2,128,32]{3,2,1,0:T(8,128)S(1)} %get-tuple-element.19.left_ref, f32[4,2,32,128]{3,2,1,0:T(8,128)S(1)} %get-tuple-element.20.right_ref, bf16[5,1,4,2,8,16384]{5,4,3,2,1,0:T(8,128)(2,1)S(1)} %copy-done), custom_call_target="tpu_custom_call" | custom-call | flops 33554432 | bytes 2097152 | tf_op jit(solution)/shard_map/forward/pallas_call | solution.py:294
  38.9 1.6 %collective-permute-start = (bf16[2,8,128,128]{3,2,1,0:T(8,128)(2,1)S(1)}, bf16[2,8,128,128]{3,2,1,0:T(8,128)(2,1)S(1)}, u32[]{:S(2)}, u32[]{:S(2)}) collective-permute-start(bf16[2,8,128,128]{3,2,1,0:T(8,128)(2,1)S(1)} %forward.5.own_ref), channel_id=1, source_target_pairs={{0,2},{2,0},{1,3},{3,1},{4,6},{6,4},{5,7},{7,5},{8,10},{10,8},{9,1... | collective-permute-start | bytes 1572872 | tf_op jit(solution)/shard_map/ppermute | solution.py:358
  41.1 0.0 copy-done.3
  41.2 0.1 fusion.weights
  41.2 0.0 collective-permute-done.4.other_ref
  41.2 0.0 copy-done.1
  41.2 10.7 %backward.5 = (bf16[5,1,2,8,16384]{4,3,2,1,0:T(8,128)(2,1)}, f32[2,32,128]{2,1,0:T(8,128)S(1)}, f32[2,32,128]{2,1,0:T(8,128)S(1)}) custom-call(s32[5,2]{1,0:T(8,128)S(1)} %copy.20.blocks, s32[1]{0:T(128)S(6)} %copy.26.counts, f32[4,2,128,32]{3,2,1,0:T(8,128)S(1)} %get-tuple-element.19.left_ref, f32[4,2,32,128]{3,2,1,0:T(8,128)S(1)} %get-tuple-element.20.right_ref, ...), custom_call_target="tpu_custom_call" | custom-call | flops 67108864 | bytes 2097152 | tf_op jit(solution)/shard_map/backward/pallas_call | solution.py:317
  51.9 0.0 collective-permute-done.3.other_ref
  51.9 10.6 %backward.6 = (bf16[5,1,2,8,16384]{4,3,2,1,0:T(8,128)(2,1)}, f32[2,32,128]{2,1,0:T(8,128)S(1)}, f32[2,32,128]{2,1,0:T(8,128)S(1)}) custom-call(s32[5,2]{1,0:T(8,128)S(1)} %copy.20.blocks, s32[1]{0:T(128)S(6)} %copy.26.counts, f32[4,2,128,32]{3,2,1,0:T(8,128)S(1)} %get-tuple-element.19.left_ref, ...), custom_call_target="tpu_custom_call", output_to_operand_aliasing={{0}: (8, {})} | custom-call | flops 67108864 | bytes 2097152 | tf_op jit(solution)/shard_map/backward/pallas_call | solution.py:317
  62.5 0.0 collective-permute-done.2.other_ref
  62.5 10.6 %backward.7 = (bf16[5,1,2,8,16384]{4,3,2,1,0:T(8,128)(2,1)}, f32[2,32,128]{2,1,0:T(8,128)S(1)}, f32[2,32,128]{2,1,0:T(8,128)S(1)}) custom-call(s32[5,2]{1,0:T(8,128)S(1)} %copy.20.blocks, s32[1]{0:T(128)S(6)} %copy.26.counts, f32[4,2,128,32]{3,2,1,0:T(8,128)S(1)} %get-tuple-element.19.left_ref, ...), custom_call_target="tpu_custom_call", output_to_operand_aliasing={{0}: (8, {})} | custom-call | flops 67108864 | bytes 2097152 | tf_op jit(solution)/shard_map/backward/pallas_call | solution.py:317
  73.2 0.0 collective-permute-done.1.other_ref
  73.2 10.6 %backward.8 = (bf16[5,1,2,8,16384]{4,3,2,1,0:T(8,128)(2,1)}, f32[2,32,128]{2,1,0:T(8,128)S(1)}, f32[2,32,128]{2,1,0:T(8,128)S(1)}) custom-call(s32[5,2]{1,0:T(8,128)S(1)} %copy.20.blocks, s32[1]{0:T(128)S(6)} %copy.26.counts, f32[4,2,128,32]{3,2,1,0:T(8,128)S(1)} %get-tuple-element.19.left_ref, ...), custom_call_target="tpu_custom_call", output_to_operand_aliasing={{0}: (8, {})} | custom-call | flops 67108864 | bytes 2097152 | tf_op jit(solution)/shard_map/backward/pallas_call | solution.py:317
  83.8 0.0 collective-permute-done.other_ref
  83.8 10.6 %backward.9 = (bf16[5,1,2,8,16384]{4,3,2,1,0:T(8,128)(2,1)}, f32[2,32,128]{2,1,0:T(8,128)S(1)}, f32[2,32,128]{2,1,0:T(8,128)S(1)}) custom-call(s32[5,2]{1,0:T(8,128)S(1)} %copy.20.blocks, s32[1]{0:T(128)S(6)} %copy.26.counts, f32[4,2,128,32]{3,2,1,0:T(8,128)S(1)} %get-tuple-element.19.left_ref, ...), custom_call_target="tpu_custom_call", output_to_operand_aliasing={{0}: (8, {})} | custom-call | flops 67108864 | bytes 2097152 | tf_op jit(solution)/shard_map/backward/pallas_call | solution.py:317
  94.5 7.8 %reduce_gradient.1 = f32[4,2,8,64]{3,2,1,0:T(8,128)S(1)} custom-call(f32[2,5,4]{2,1,0:T(8,128)S(1)} %fusion.weights, f32[2,32,128]{2,1,0:T(8,128)S(1)} %get-tuple-element.26.refs_0_, f32[2,32,128]{2,1,0:T(8,128)S(1)} %get-tuple-element.27.refs_1_, f32[2,32,128]{2,1,0:T(8,128)S(1)} %get-tuple-element.28.refs_2_, f32[2,32,128]{2,1,0:T(8,128)S(1)} %get-tuple-element.29.refs_3_, ...), custom_call_target="tpu_custom_call" | custom-call | tf_op jit(solution)/shard_map/reduce_gradient/pallas_call | solution.py:368
  102.3 0.6 copy.27
Async XLA Ops:
  0.6 0.8 copy-start.2
  10.8 4.0 %copy-start = (bf16[5,1,4,2,8,16384]{5,4,3,2,1,0:T(8,128)(2,1)S(1)}, bf16[5,1,4,2,8,16384]{5,4,3,2,1,0:T(8,128)(2,1)}, u32[]{:S(2)}) copy-start(bf16[5,1,4,2,8,16384]{5,4,3,2,1,0:T(8,128)(2,1)} %coh_ref.19) | copy-start | bytes 31457284
  18.7 22.5 %collective-permute-start.4 = (bf16[2,8,128,128]{3,2,1,0:T(8,128)(2,1)S(1)}, bf16[2,8,128,128]{3,2,1,0:T(8,128)(2,1)S(1)}, u32[]{:S(2)}, u32[]{:S(2)}) collective-permute-start(bf16[2,8,128,128]{3,2,1,0:T(8,128)(2,1)S(1)} %forward.9.own_ref), channel_id=1, source_target_pairs={{0,2},{2,0},{1,3},{3,1},{4,6},{6,4},{5,7},{7,5},{8,10},{10,8},{9,1... | collective-permute-start | bytes 1572872 | tf_op jit(solution)/shard_map/ppermute | solution.py:358
  24.3 27.6 %collective-permute-start.3 = (bf16[2,8,128,128]{3,2,1,0:T(8,128)(2,1)S(1)}, bf16[2,8,128,128]{3,2,1,0:T(8,128)(2,1)S(1)}, u32[]{:S(2)}, u32[]{:S(2)}) collective-permute-start(bf16[2,8,128,128]{3,2,1,0:T(8,128)(2,1)S(1)} %forward.8.own_ref), channel_id=1, source_target_pairs={{0,2},{2,0},{1,3},{3,1},{4,6},{6,4},{5,7},{7,5},{8,10},{10,8},{9,1... | collective-permute-start | bytes 1572872 | tf_op jit(solution)/shard_map/ppermute | solution.py:358
  28.8 33.7 %collective-permute-start.2 = (bf16[2,8,128,128]{3,2,1,0:T(8,128)(2,1)S(1)}, bf16[2,8,128,128]{3,2,1,0:T(8,128)(2,1)S(1)}, u32[]{:S(2)}, u32[]{:S(2)}) collective-permute-start(bf16[2,8,128,128]{3,2,1,0:T(8,128)(2,1)S(1)} %forward.7.own_ref), channel_id=1, source_target_pairs={{0,2},{2,0},{1,3},{3,1},{4,6},{6,4},{5,7},{7,5},{8,10},{10,8},{9,1... | collective-permute-start | bytes 1572872 | tf_op jit(solution)/shard_map/ppermute | solution.py:358
  34.3 6.8 %copy-start.3 = (s32[5,2]{0,1:T(2,128)S(1)}, s32[5,2]{0,1:T(2,128)}, u32[]{:S(2)}) copy-start(s32[5,2]{0,1:T(2,128)} %param.5) | copy-start | bytes 124
  34.4 6.9 %copy-start.1 = (bf16[5,1,2,8,16384]{4,3,2,1,0:T(8,128)(2,1)S(1)}, bf16[5,1,2,8,16384]{4,3,2,1,0:T(8,128)(2,1)}, u32[]{:S(2)}) copy-start(bf16[5,1,2,8,16384]{4,3,2,1,0:T(8,128)(2,1)} %obs_ref.9) | copy-start | bytes 7864324
  34.4 38.8 %collective-permute-start.1 = (bf16[2,8,128,128]{3,2,1,0:T(8,128)(2,1)S(1)}, bf16[2,8,128,128]{3,2,1,0:T(8,128)(2,1)S(1)}, u32[]{:S(2)}, u32[]{:S(2)}) collective-permute-start(bf16[2,8,128,128]{3,2,1,0:T(8,128)(2,1)S(1)} %forward.6.own_ref), channel_id=1, source_target_pairs={{0,2},{2,0},{1,3},{3,1},{4,6},{6,4},{5,7},{7,5},{8,10},{10,8},{9,1... | collective-permute-start | bytes 1572872 | tf_op jit(solution)/shard_map/ppermute | solution.py:358
  38.9 44.9 %collective-permute-start = (bf16[2,8,128,128]{3,2,1,0:T(8,128)(2,1)S(1)}, bf16[2,8,128,128]{3,2,1,0:T(8,128)(2,1)S(1)}, u32[]{:S(2)}, u32[]{:S(2)}) collective-permute-start(bf16[2,8,128,128]{3,2,1,0:T(8,128)(2,1)S(1)} %forward.5.own_ref), channel_id=1, source_target_pairs={{0,2},{2,0},{1,3},{3,1},{4,6},{6,4},{5,7},{7,5},{8,10},{10,8},{9,1... | collective-permute-start | bytes 1572872 | tf_op jit(solution)/shard_map/ppermute | solution.py:358

commit v3 on v2

--- a/solution.py
+++ b/solution.py
@@ -165,7 +165,7 @@
         copy.wait_send()
 
 
-def forward_kernel(dirs, blocks, left_ref, right_ref, coh_ref, out_ref, wide):
+def forward_kernel(dirs, blocks, left_ref, right_ref, coh_ref, out_ref, kept_ref, wide):
     blk = left_ref.shape[2]
 
     @pl.loop(0, blk // 16)
@@ -177,17 +177,21 @@
                 wide,
                 k * 128,
             )
-        halves = []
-        for h in range(2):
-            rows = left_ref[0, 0, pl.ds(p0 + h * 8, 8), :]
-            total = None
-            for k in range(dirs):
+        halves = [None, None]
+        for k in range(dirs):
+            lefts = []
+            for h in range(2):
+                rows = left_ref[0, 0, pl.ds(p0 + h * 8, 8), :]
                 model = parts_at(wide, k * 128 + h * 64)
                 jq = [right_ref[0, 0, k * 8 + c : k * 8 + c + 1, :] for c in range(8)]
                 jp = [rows[:, k * 8 + c : k * 8 + c + 1] for c in range(8)]
-                term = product(jp, product_adj_right(model, jq))
-                total = term if total is None else [x + y for x, y in zip(total, term)]
-            halves.append(total)
+                left = product(jp, model)
+                lefts.append(left)
+                term = product_adj_right(left, jq)
+                halves[h] = term if k == 0 else [x + y for x, y in zip(halves[h], term)]
+            for c in range(8):
+                both = jnp.concatenate([lefts[0][c], lefts[1][c]], axis=0)
+                kept_ref[0, k, c, pl.ds(p0, 16), :] = both.astype(jnp.bfloat16)
         for c in range(8):
             both = jnp.concatenate([halves[0][c], halves[1][c]], axis=0)
             out_ref[0, c, pl.ds(p0, 16), :] = both.astype(jnp.bfloat16)
@@ -198,16 +202,16 @@
     slot,
     blocks,
     counts,
-    left_ref,
     right_ref,
     own_ref,
     other_ref,
+    kept_ref,
     obs_ref,
     coh_ref,
     *refs,
 ):
     res_ref, first_ref, second_ref, wide, wide_obs, acc, sums_first = refs[-7:]
-    blk = left_ref.shape[2]
+    blk = right_ref.shape[3]
     used = slot < counts[0]
     off_diag = blocks[slot, 0] < blocks[slot, 1]
     acc[...] = jnp.zeros_like(acc)
@@ -241,24 +245,38 @@
             res_ref[0, 0, 0, :, lanes(p)] = wide_obs[p * 8 : p * 8 + 8, :].astype(jnp.bfloat16)
         for k in range(dirs):
             total = None
+            firsts = []
+            kept = [kept_ref[0, k, c, pl.ds(p0, 16), :].astype(jnp.float32) for c in range(8)]
             for h in range(2):
                 model = parts_at(wide, k * 128 + h * 64)
                 resid = [r[h * 8 : h * 8 + 8] for r in rest]
                 jq = [right_ref[0, 0, k * 8 + c : k * 8 + c + 1, :] for c in range(8)]
-                rows = left_ref[0, 0, pl.ds(p0 + h * 8, 8), :]
-                jp = [rows[:, k * 8 + c : k * 8 + c + 1] for c in range(8)]
-                toward_first = product_adj_right(resid, product_adj_right(model, jq))
-                for c in range(8):
-                    sums_first[pl.ds(p0 + h * 8, 8), k * 8 + c : k * 8 + c + 1] = jnp.sum(
-                        toward_first[c], axis=1, keepdims=True
-                    )
-                toward_second = product_adj_left(resid, product(jp, model))
+                firsts.append(product_adj_right(resid, product_adj_right(model, jq)))
+                toward_second = product_adj_left(resid, [y[h * 8 : h * 8 + 8] for y in kept])
                 total = toward_second if h == 0 else [x + y for x, y in zip(total, toward_second)]
             for c in range(8):
                 acc[k * 8 + c] += total[c]
+            rows = [firsts[h][c] for c in range(8) for h in range(2)]
+            stack = jnp.concatenate(rows, axis=0).astype(jnp.bfloat16)
+            summed = lax.dot_general(
+                jnp.ones((8, LANES), jnp.bfloat16),
+                stack,
+                (((1,), (1,)), ((), ())),
+                preferred_element_type=jnp.float32,
+            )
+            sums_first[k, pl.ds(g, 1), :] = summed[:1]
 
     second_ref[0] = jnp.sum(acc[...], axis=1)
-    first_ref[0] = jnp.transpose(sums_first[...])[: dirs * 8]
+    row = lax.broadcasted_iota(jnp.int32, (8, LANES), 0)
+    col = lax.broadcasted_iota(jnp.int32, (8, LANES), 1)
+    apart = (col // 16 - row) & 7
+    for k in range(dirs):
+        source = sums_first[k]
+        result = source
+        for d in range(1, 8):
+            moved = pltpu.roll(pltpu.roll(source, 8 - d, 0), 16 * d, 1)
+            result = jnp.where(apart == d, moved, result)
+        first_ref[0, k * 8 : k * 8 + 8, :] = result
 
 
 def fast_body(blocks, counts, gains, coherency, observed):
@@ -301,10 +319,16 @@
                     pl.BlockSpec((1, 1, comps, blk), lambda f, b: (b[slot, 1], f, 0, 0)),
                     pl.BlockSpec((1, 1, dirs, 1, 8, base), lambda f, b: (slot, 0, 0, f, 0, 0)),
                 ],
-                out_specs=pl.BlockSpec((1, 8, blk, LANES), lambda f, b: (f, 0, 0, 0)),
+                out_specs=[
+                    pl.BlockSpec((1, 8, blk, LANES), lambda f, b: (f, 0, 0, 0)),
+                    pl.BlockSpec((1, dirs, 8, blk, LANES), lambda f, b: (f, 0, 0, 0, 0)),
+                ],
                 scratch_shapes=[pltpu.VMEM((dirs * 128, LANES), jnp.float32)],
             ),
-            out_shape=jax.ShapeDtypeStruct((chans, 8, blk, blk), jnp.bfloat16),
+            out_shape=[
+                jax.ShapeDtypeStruct((chans, 8, blk, blk), jnp.bfloat16),
+                jax.ShapeDtypeStruct((chans, dirs, 8, blk, blk), jnp.bfloat16),
+            ],
             compiler_params=kind,
             cost_estimate=pl.CostEstimate(
                 flops=4 * ops, bytes_accessed=dirs * chans * 8 * base * 2, transcendentals=0
@@ -312,7 +336,7 @@
             name="forward",
         )(blocks, left, right, coherency)
 
-    def backward(slot, own, other, residual):
+    def backward(slot, own, other, kept, residual):
         held = [] if residual is None else [residual]
         return pl.pallas_call(
             functools.partial(backward_kernel, dirs, slot),
@@ -320,10 +344,10 @@
                 num_scalar_prefetch=2,
                 grid=(chans,),
                 in_specs=[
-                    pl.BlockSpec((1, 1, blk, comps), lambda f, b, n: (b[slot, 0], f, 0, 0)),
                     pl.BlockSpec((1, 1, comps, blk), lambda f, b, n: (b[slot, 1], f, 0, 0)),
                     pl.BlockSpec((1, 8, blk, LANES), lambda f, b, n: (f, 0, 0, 0)),
                     pl.BlockSpec((1, 8, blk, LANES), lambda f, b, n: (f, 0, 0, 0)),
+                    pl.BlockSpec((1, dirs, 8, blk, LANES), lambda f, b, n: (f, 0, 0, 0, 0)),
                     pl.BlockSpec((1, 1, 1, 8, base), lambda f, b, n: (slot, 0, f, 0, 0)),
                     pl.BlockSpec((1, 1, dirs, 1, 8, base), lambda f, b, n: (slot, 0, 0, f, 0, 0)),
                 ]
@@ -337,7 +361,7 @@
                     pltpu.VMEM((dirs * 128, LANES), jnp.float32),
                     pltpu.VMEM((128, LANES), jnp.float32),
                     pltpu.VMEM((comps, 8, LANES), jnp.float32),
-                    pltpu.VMEM((blk, LANES), jnp.float32),
+                    pltpu.VMEM((dirs, 8, LANES), jnp.float32),
                 ],
             ),
             out_shape=[
@@ -351,15 +375,15 @@
                 flops=8 * ops, bytes_accessed=dirs * chans * 8 * base * 2, transcendentals=0
             ),
             name="backward",
-        )(blocks, counts, left, right, own, other, observed, coherency, *held)
+        )(blocks, counts, right, own, other, kept, observed, coherency, *held)
 
     swap = [(0, 1), (1, 0)]
-    own = [forward(slot) for slot in range(maxb)]
+    own, kept = zip(*[forward(slot) for slot in range(maxb)])
     other = [lax.ppermute(x, "dir", swap) for x in own]
     residual = None
     firsts, seconds = [], []
     for slot in range(maxb):
-        residual, first, second = backward(slot, own[slot], other[slot], residual)
+        residual, first, second = backward(slot, own[slot], other[slot], kept[slot], residual)
         firsts.append(first)
         seconds.append(second)
     index = jnp.arange(nblocks)

time: 103 us -> 94.6 us (0.918)
  Pallas kernels: 89.5 us -> 80.8 us
    pallas_call x5, Pallas kernels: 53.2 us -> 41.8 us  [backward(): pl.pallas_call(functools.partial(backward_kernel, dirs, slot), grid_spec=...]
    pallas_call x5, Pallas kernels: 19.8 us -> 22.6 us  [forward(): pl.pallas_call(functools.partial(forward_kernel, dirs), grid_spec=pltpu.P...]
    unnamed x10 -> x16, local copies, waits for them, and re-layouts: 6.13 us -> 6.14 us
  transfers between devices with their start and end apart: 5 -> 5, of which waited for: 0 -> 0; matrix products, arithmetic and copies ran while one was open for 0% -> 0% of each run, Pallas kernels for 57% -> 55%
where the time goes in v3:
time: 94.6 us; the launch traced here: 94.3 us
  Pallas kernels  80.8 us (85%)
  local copies, waits for them, and re-layouts  6.14 us (6%)
  starting transfers between devices  5.87 us (6%)
  between operations  1.42 us (2%)
    pallas_call x5, Pallas kernels, backward(): pl.pallas_call(functools.partial(backward_kernel, dirs, slot), grid_spec=...  41.8 us
    pallas_call x5, Pallas kernels, forward(): pl.pallas_call(functools.partial(forward_kernel, dirs), grid_spec=pltpu.P...  22.6 us
    pallas_call x1, Pallas kernels, fast_body(): pl.pallas_call(functools.partial(gather_kernel, nblocks), out_shape=[jax....  8.62 us
    pallas_call x1, Pallas kernels, fast_body(): pl.pallas_call(functools.partial(reduce_kernel, nblocks, npol), out_shape...  7.83 us
    unnamed x16, local copies, waits for them, and re-layouts  6.14 us
    ppermute x5, starting transfers between devices, fast_body(): other = [lax.ppermute(x, 'dir', swap) for x in own]  5.87 us
  transfers between devices with their start and end apart: 5, of which 0 were waited for; matrix products, arithmetic and copies ran while one was open for 0% of the time, Pallas kernels for 55%

profile of v3, /device:TPU:0, one launch (start us, length us, event | category | flops | bytes accessed | tf_op | source)
XLA Modules:
  0.0 94.3 jit_solution(9210207547008935998)
XLA Ops:
  0.6 0.0 copy-start.2
  0.6 0.7 copy-done.2
  1.4 8.6 %gather_gains.1 = (f32[4,2,128,32]{3,2,1,0:T(8,128)S(1)}, f32[4,2,32,128]{3,2,1,0:T(8,128)S(1)}) custom-call(f32[4,2,8,128]{3,2,1,0:T(8,128)S(1)} %copy-done.2), custom_call_target="tpu_custom_call" | custom-call | tf_op jit(solution)/shard_map/gather_gains/pallas_call | solution.py:290
  10.0 0.8 copy.20.blocks
  10.8 0.0 copy-start
  10.8 4.0 %copy-done = bf16[5,1,4,2,8,16384]{5,4,3,2,1,0:T(8,128)(2,1)S(1)} copy-done((bf16[5,1,4,2,8,16384]{5,4,3,2,1,0:T(8,128)(2,1)S(1)}, bf16[5,1,4,2,8,16384]{5,4,3,2,1,0:T(8,128)(2,1)}, u32[]{:S(2)}) %copy-start) | copy-done | bytes 10485784
  14.8 4.5 %forward.9 = (bf16[2,8,128,128]{3,2,1,0:T(8,128)(2,1)S(1)}, bf16[2,4,8,128,128]{4,3,2,1,0:T(8,128)(2,1)S(1)}) custom-call(s32[5,2]{1,0:T(8,128)S(1)} %copy.20.blocks, f32[4,2,128,32]{3,2,1,0:T(8,128)S(1)} %get-tuple-element.30.left_ref, f32[4,2,32,128]{3,2,1,0:T(8,128)S(1)} %get-tuple-element.29.right_ref, bf16[5,1,4,2,8,16384]{5,4,3,2,1,0:T(8,128)(2,1)S(1)} %copy-done), custom_call_target="tpu_custom_call" | custom-call | flops 33554432 | bytes 2097152 | tf_op jit(solution)/shard_map/forward/pallas_call | solution.py:312
  19.3 1.6 %collective-permute-start.4 = (bf16[2,8,128,128]{3,2,1,0:T(8,128)(2,1)S(1)}, bf16[2,8,128,128]{3,2,1,0:T(8,128)(2,1)S(1)}, u32[]{:S(2)}, u32[]{:S(2)}) collective-permute-start(bf16[2,8,128,128]{3,2,1,0:T(8,128)(2,1)S(1)} %get-tuple-element.39.own_ref), channel_id=1, source_target_pairs={{0,2},{2,0},{1,3},{3,1},{4,6},{6,4},{5,7},{7,5},{8,10},{10,8},{9,1... | collective-permute-start | bytes 1572872 | tf_op jit(solution)/shard_map/ppermute | solution.py:382
  20.8 4.5 %forward.8 = (bf16[2,8,128,128]{3,2,1,0:T(8,128)(2,1)S(1)}, bf16[2,4,8,128,128]{4,3,2,1,0:T(8,128)(2,1)S(1)}) custom-call(s32[5,2]{1,0:T(8,128)S(1)} %copy.20.blocks, f32[4,2,128,32]{3,2,1,0:T(8,128)S(1)} %get-tuple-element.30.left_ref, f32[4,2,32,128]{3,2,1,0:T(8,128)S(1)} %get-tuple-element.29.right_ref, bf16[5,1,4,2,8,16384]{5,4,3,2,1,0:T(8,128)(2,1)S(1)} %copy-done), custom_call_target="tpu_custom_call" | custom-call | flops 33554432 | bytes 2097152 | tf_op jit(solution)/shard_map/forward/pallas_call | solution.py:312
  25.4 0.6 collective-permute-start.3
  26.0 4.5 %forward.7 = (bf16[2,8,128,128]{3,2,1,0:T(8,128)(2,1)S(1)}, bf16[2,4,8,128,128]{4,3,2,1,0:T(8,128)(2,1)S(1)}) custom-call(s32[5,2]{1,0:T(8,128)S(1)} %copy.20.blocks, f32[4,2,128,32]{3,2,1,0:T(8,128)S(1)} %get-tuple-element.30.left_ref, f32[4,2,32,128]{3,2,1,0:T(8,128)S(1)} %get-tuple-element.29.right_ref, bf16[5,1,4,2,8,16384]{5,4,3,2,1,0:T(8,128)(2,1)S(1)} %copy-done), custom_call_target="tpu_custom_call" | custom-call | flops 33554432 | bytes 2097152 | tf_op jit(solution)/shard_map/forward/pallas_call | solution.py:312
  30.5 1.6 %collective-permute-start.2 = (bf16[2,8,128,128]{3,2,1,0:T(8,128)(2,1)S(1)}, bf16[2,8,128,128]{3,2,1,0:T(8,128)(2,1)S(1)}, u32[]{:S(2)}, u32[]{:S(2)}) collective-permute-start(bf16[2,8,128,128]{3,2,1,0:T(8,128)(2,1)S(1)} %get-tuple-element.35.own_ref), channel_id=1, source_target_pairs={{0,2},{2,0},{1,3},{3,1},{4,6},{6,4},{5,7},{7,5},{8,10},{10,8},{9,1... | collective-permute-start | bytes 1572872 | tf_op jit(solution)/shard_map/ppermute | solution.py:382
  32.0 0.0 slice-start
  32.0 0.0 slice-start.1
  32.1 4.5 %forward.6 = (bf16[2,8,128,128]{3,2,1,0:T(8,128)(2,1)S(1)}, bf16[2,4,8,128,128]{4,3,2,1,0:T(8,128)(2,1)S(1)}) custom-call(s32[5,2]{1,0:T(8,128)S(1)} %copy.20.blocks, f32[4,2,128,32]{3,2,1,0:T(8,128)S(1)} %get-tuple-element.30.left_ref, f32[4,2,32,128]{3,2,1,0:T(8,128)S(1)} %get-tuple-element.29.right_ref, bf16[5,1,4,2,8,16384]{5,4,3,2,1,0:T(8,128)(2,1)S(1)} %copy-done), custom_call_target="tpu_custom_call" | custom-call | flops 33554432 | bytes 2097152 | tf_op jit(solution)/shard_map/forward/pallas_call | solution.py:312
  36.6 0.0 copy-start.3
  36.6 0.0 slice-start.2
  36.6 0.0 copy-start.1
  36.6 0.6 collective-permute-start.1
  37.2 4.5 %forward.5 = (bf16[2,8,128,128]{3,2,1,0:T(8,128)(2,1)S(1)}, bf16[2,4,8,128,128]{4,3,2,1,0:T(8,128)(2,1)S(1)}) custom-call(s32[5,2]{1,0:T(8,128)S(1)} %copy.20.blocks, f32[4,2,128,32]{3,2,1,0:T(8,128)S(1)} %get-tuple-element.30.left_ref, f32[4,2,32,128]{3,2,1,0:T(8,128)S(1)} %get-tuple-element.29.right_ref, bf16[5,1,4,2,8,16384]{5,4,3,2,1,0:T(8,128)(2,1)S(1)} %copy-done), custom_call_target="tpu_custom_call" | custom-call | flops 33554432 | bytes 2097152 | tf_op jit(solution)/shard_map/forward/pallas_call | solution.py:312
  41.7 1.6 %collective-permute-start = (bf16[2,8,128,128]{3,2,1,0:T(8,128)(2,1)S(1)}, bf16[2,8,128,128]{3,2,1,0:T(8,128)(2,1)S(1)}, u32[]{:S(2)}, u32[]{:S(2)}) collective-permute-start(bf16[2,8,128,128]{3,2,1,0:T(8,128)(2,1)S(1)} %get-tuple-element.31.own_ref), channel_id=1, source_target_pairs={{0,2},{2,0},{1,3},{3,1},{4,6},{6,4},{5,7},{7,5},{8,10},{10,8},{9,1... | collective-permute-start | bytes 1572872 | tf_op jit(solution)/shard_map/ppermute | solution.py:382
  43.9 0.0 copy-done.3
  44.0 0.1 fusion.weights
  44.0 0.0 collective-permute-done.4.other_ref
  44.0 0.0 slice-done
  44.0 0.0 slice-done.1
  44.0 0.0 slice-done.2
  44.1 0.0 copy-done.1
  44.1 8.4 %backward.5 = (bf16[5,1,2,8,16384]{4,3,2,1,0:T(8,128)(2,1)}, f32[2,32,128]{2,1,0:T(8,128)S(1)}, f32[2,32,128]{2,1,0:T(8,128)S(1)}) custom-call(s32[5,2]{1,0:T(8,128)S(1)} %copy.20.blocks, s32[1]{0:T(128)S(6)} %copy.26.counts, f32[4,2,32,128]{3,2,1,0:T(8,128)S(1)} %get-tuple-element.29.right_ref, bf16[2,8,128,128]{3,2,1,0:T(8,128)(2,1)S(1)} %get-tuple-element.39.own_ref, ...), custom_call_target="tpu_custom_call" | custom-call | flops 67108864 | bytes 2097152 | tf_op jit(solution)/shard_map/backward/pallas_call | solution.py:341
  52.4 0.0 collective-permute-done.3.other_ref
  52.4 8.4 %backward.6 = (bf16[5,1,2,8,16384]{4,3,2,1,0:T(8,128)(2,1)}, f32[2,32,128]{2,1,0:T(8,128)S(1)}, f32[2,32,128]{2,1,0:T(8,128)S(1)}) custom-call(s32[5,2]{1,0:T(8,128)S(1)} %copy.20.blocks, s32[1]{0:T(128)S(6)} %copy.26.counts, f32[4,2,32,128]{3,2,1,0:T(8,128)S(1)} %get-tuple-element.29.right_ref, ...), custom_call_target="tpu_custom_call", output_to_operand_aliasing={{0}: (8, {})} | custom-call | flops 67108864 | bytes 2097152 | tf_op jit(solution)/shard_map/backward/pallas_call | solution.py:341
  60.8 0.0 collective-permute-done.2.other_ref
  60.8 8.4 %backward.7 = (bf16[5,1,2,8,16384]{4,3,2,1,0:T(8,128)(2,1)}, f32[2,32,128]{2,1,0:T(8,128)S(1)}, f32[2,32,128]{2,1,0:T(8,128)S(1)}) custom-call(s32[5,2]{1,0:T(8,128)S(1)} %copy.20.blocks, s32[1]{0:T(128)S(6)} %copy.26.counts, f32[4,2,32,128]{3,2,1,0:T(8,128)S(1)} %get-tuple-element.29.right_ref, ...), custom_call_target="tpu_custom_call", output_to_operand_aliasing={{0}: (8, {})} | custom-call | flops 67108864 | bytes 2097152 | tf_op jit(solution)/shard_map/backward/pallas_call | solution.py:341
  69.1 0.0 collective-permute-done.1.other_ref
  69.2 8.4 %backward.8 = (bf16[5,1,2,8,16384]{4,3,2,1,0:T(8,128)(2,1)}, f32[2,32,128]{2,1,0:T(8,128)S(1)}, f32[2,32,128]{2,1,0:T(8,128)S(1)}) custom-call(s32[5,2]{1,0:T(8,128)S(1)} %copy.20.blocks, s32[1]{0:T(128)S(6)} %copy.26.counts, f32[4,2,32,128]{3,2,1,0:T(8,128)S(1)} %get-tuple-element.29.right_ref, ...), custom_call_target="tpu_custom_call", output_to_operand_aliasing={{0}: (8, {})} | custom-call | flops 67108864 | bytes 2097152 | tf_op jit(solution)/shard_map/backward/pallas_call | solution.py:341
  77.5 0.0 collective-permute-done.other_ref
  77.5 8.4 %backward.9 = (bf16[5,1,2,8,16384]{4,3,2,1,0:T(8,128)(2,1)}, f32[2,32,128]{2,1,0:T(8,128)S(1)}, f32[2,32,128]{2,1,0:T(8,128)S(1)}) custom-call(s32[5,2]{1,0:T(8,128)S(1)} %copy.20.blocks, s32[1]{0:T(128)S(6)} %copy.26.counts, f32[4,2,32,128]{3,2,1,0:T(8,128)S(1)} %get-tuple-element.29.right_ref, ...), custom_call_target="tpu_custom_call", output_to_operand_aliasing={{0}: (8, {})} | custom-call | flops 67108864 | bytes 2097152 | tf_op jit(solution)/shard_map/backward/pallas_call | solution.py:341
  85.9 7.8 %reduce_gradient.1 = f32[4,2,8,64]{3,2,1,0:T(8,128)S(1)} custom-call(f32[2,5,4]{2,1,0:T(8,128)S(1)} %fusion.weights, f32[2,32,128]{2,1,0:T(8,128)S(1)} %get-tuple-element.46.refs_0_, f32[2,32,128]{2,1,0:T(8,128)S(1)} %get-tuple-element.47.refs_1_, f32[2,32,128]{2,1,0:T(8,128)S(1)} %get-tuple-element.48.refs_2_, f32[2,32,128]{2,1,0:T(8,128)S(1)} %get-tuple-element.49.refs_3_, ...), custom_call_target="tpu_custom_call" | custom-call | tf_op jit(solution)/shard_map/reduce_gradient/pallas_call | solution.py:392
  93.7 0.6 copy.27
  (1 shorter events, 0.0 us)
Async XLA Ops:
  0.6 0.8 copy-start.2
  10.8 4.0 %copy-start = (bf16[5,1,4,2,8,16384]{5,4,3,2,1,0:T(8,128)(2,1)S(1)}, bf16[5,1,4,2,8,16384]{5,4,3,2,1,0:T(8,128)(2,1)}, u32[]{:S(2)}) copy-start(bf16[5,1,4,2,8,16384]{5,4,3,2,1,0:T(8,128)(2,1)} %coh_ref.19) | copy-start | bytes 31457284
  19.3 24.7 %collective-permute-start.4 = (bf16[2,8,128,128]{3,2,1,0:T(8,128)(2,1)S(1)}, bf16[2,8,128,128]{3,2,1,0:T(8,128)(2,1)S(1)}, u32[]{:S(2)}, u32[]{:S(2)}) collective-permute-start(bf16[2,8,128,128]{3,2,1,0:T(8,128)(2,1)S(1)} %get-tuple-element.39.own_ref), channel_id=1, source_target_pairs={{0,2},{2,0},{1,3},{3,1},{4,6},{6,4},{5,7},{7,5},{8,10},{10,8},{9,1... | collective-permute-start | bytes 1572872 | tf_op jit(solution)/shard_map/ppermute | solution.py:382
  25.4 27.1 %collective-permute-start.3 = (bf16[2,8,128,128]{3,2,1,0:T(8,128)(2,1)S(1)}, bf16[2,8,128,128]{3,2,1,0:T(8,128)(2,1)S(1)}, u32[]{:S(2)}, u32[]{:S(2)}) collective-permute-start(bf16[2,8,128,128]{3,2,1,0:T(8,128)(2,1)S(1)} %get-tuple-element.37.own_ref), channel_id=1, source_target_pairs={{0,2},{2,0},{1,3},{3,1},{4,6},{6,4},{5,7},{7,5},{8,10},{10,8},{9,1... | collective-permute-start | bytes 1572872 | tf_op jit(solution)/shard_map/ppermute | solution.py:382
  30.5 30.3 %collective-permute-start.2 = (bf16[2,8,128,128]{3,2,1,0:T(8,128)(2,1)S(1)}, bf16[2,8,128,128]{3,2,1,0:T(8,128)(2,1)S(1)}, u32[]{:S(2)}, u32[]{:S(2)}) collective-permute-start(bf16[2,8,128,128]{3,2,1,0:T(8,128)(2,1)S(1)} %get-tuple-element.35.own_ref), channel_id=1, source_target_pairs={{0,2},{2,0},{1,3},{3,1},{4,6},{6,4},{5,7},{7,5},{8,10},{10,8},{9,1... | collective-permute-start | bytes 1572872 | tf_op jit(solution)/shard_map/ppermute | solution.py:382
  32.0 12.0 %slice-start = ((s8[10485760]{0:T(1024)(128)(4,1)}), s8[4194304]{0:T(1024)(128)(4,1)S(1)}, s32[]{:S(2)}) async-start(s8[10485760]{0:T(1024)(128)(4,1)} %bitcast.1), calls=%async_computation | async-start | bytes 8388608
  32.0 12.0 %slice-start.1 = ((s8[10485760]{0:T(1024)(128)(4,1)}), s8[4194304]{0:T(1024)(128)(4,1)S(1)}, s32[]{:S(2)}) async-start(s8[10485760]{0:T(1024)(128)(4,1)} %bitcast.1), calls=%async_computation.1 | async-start | bytes 8388608
  36.6 7.4 %copy-start.3 = (s32[5,2]{0,1:T(2,128)S(1)}, s32[5,2]{0,1:T(2,128)}, u32[]{:S(2)}) copy-start(s32[5,2]{0,1:T(2,128)} %param.5) | copy-start | bytes 124
  36.6 7.5 %slice-start.2 = ((s8[10485760]{0:T(1024)(128)(4,1)}), s8[2097152]{0:T(1024)(128)(4,1)S(1)}, s32[]{:S(2)}) async-start(s8[10485760]{0:T(1024)(128)(4,1)} %bitcast.1), calls=%async_computation.2 | async-start | bytes 4194304
  36.6 7.5 %copy-start.1 = (bf16[5,1,2,8,16384]{4,3,2,1,0:T(8,128)(2,1)S(1)}, bf16[5,1,2,8,16384]{4,3,2,1,0:T(8,128)(2,1)}, u32[]{:S(2)}) copy-start(bf16[5,1,2,8,16384]{4,3,2,1,0:T(8,128)(2,1)} %obs_ref.9) | copy-start | bytes 7864324
  36.6 32.5 %collective-permute-start.1 = (bf16[2,8,128,128]{3,2,1,0:T(8,128)(2,1)S(1)}, bf16[2,8,128,128]{3,2,1,0:T(8,128)(2,1)S(1)}, u32[]{:S(2)}, u32[]{:S(2)}) collective-permute-start(bf16[2,8,128,128]{3,2,1,0:T(8,128)(2,1)S(1)} %get-tuple-element.33.own_ref), channel_id=1, source_target_pairs={{0,2},{2,0},{1,3},{3,1},{4,6},{6,4},{5,7},{7,5},{8,10},{10,8},{9,1... | collective-permute-start | bytes 1572872 | tf_op jit(solution)/shard_map/ppermute | solution.py:382
  41.7 35.8 %collective-permute-start = (bf16[2,8,128,128]{3,2,1,0:T(8,128)(2,1)S(1)}, bf16[2,8,128,128]{3,2,1,0:T(8,128)(2,1)S(1)}, u32[]{:S(2)}, u32[]{:S(2)}) collective-permute-start(bf16[2,8,128,128]{3,2,1,0:T(8,128)(2,1)S(1)} %get-tuple-element.31.own_ref), channel_id=1, source_target_pairs={{0,2},{2,0},{1,3},{3,1},{4,6},{6,4},{5,7},{7,5},{8,10},{10,8},{9,1... | collective-permute-start | bytes 1572872 | tf_op jit(solution)/shard_map/ppermute | solution.py:382
